TPU v7x, 32 devices: a whole 2x2x4 slice. The times are simulated.
32 devices in a mesh: dp: 8 (over z, y), mp: 4 (over x, core).
Axes of the slice: x: 2, y: 2, z: 4, core: 2. Of those that a mesh axis runs over, the one named last changes fastest.
Arguments:
- layer_input: bfloat16 [24, 512, 768], P('dp', 'mp'), may hold values from -6 to 6
- targets: bfloat16 [24, 512, 768], P('dp', 'mp'), may hold values from -6 to 6
- attn_gain: bfloat16 [768], replicated, may hold values from 0.5 to 1.5
- ffn_gain: bfloat16 [768], replicated, may hold values from 0.5 to 1.5
- query_matrix: bfloat16 [768, 768], replicated, may hold values from -0.09375 to 0.09375
- key_matrix: bfloat16 [768, 768], replicated, may hold values from -0.09375 to 0.09375
- value_matrix: bfloat16 [768, 768], replicated, may hold values from -0.21875 to 0.21875
- attention_output_weight: bfloat16 [768, 768], replicated, may hold values from -1.25 to 1.25
- feedforward_input_weight: bfloat16 [768, 3072], replicated, may hold values from -0.21875 to 0.21875
- feedforward_output_weight: bfloat16 [3072, 768], replicated, may hold values from -0.15625 to 0.15625
- bias_table: float32 [32, 12], replicated, may hold values from -4 to 4
- factors: float32 [4, 4, 4], replicated, may hold values from -6 to 6
- down_left: float32 [4, 192], replicated, may hold values from -0.875 to 0.875
- down_right: float32 [4, 12], replicated, may hold values from -0.875 to 0.875
- up_left: float32 [4, 12], replicated, may hold values from -2 to 2
- up_right: float32 [4, 192], replicated, may hold values from -2 to 2
- lengths: int32 [24], P('dp'), may hold values from 48 to 512, as said below
- relative_bucket: int32 [512, 512], replicated, may hold values from 0 to 31, as said below
Outputs:
- loss: float32 [], replicated
- block_out: bfloat16 [24, 512, 768], P('dp', 'mp')
- grad_input: float32 [24, 512, 768], P('dp', 'mp')
- grad_attn_gain: float32 [768], replicated
- grad_ffn_gain: float32 [768], replicated
- grad_bias_table: float32 [32, 12], replicated
- grad_factors: float32 [4, 4, 4], replicated
- grad_down_left: float32 [4, 192], replicated
- grad_down_right: float32 [4, 12], replicated
- grad_up_left: float32 [4, 12], replicated
- grad_up_right: float32 [4, 192], replicated
Inputs may be any that keep to these rules, and one draw needn't show every extreme that they name: lengths[b] counts the real tokens of sequence b, which stand at its first positions; some sequence has exactly 512 of them and some exactly 48. relative_bucket[l, m] = label[t5(m - l)], where label is one permutation of 0 to 31 and t5 is T5's bidirectional bucket with max distance 128: with half = 16, exact = 8 and n = |m - l|, t5 = n for n < exact, else exact plus the number of j in 1 to half - exact - 1 with n^(half - exact) >= exact^(half - exact) * (128 / exact)^j; plus half where m > l.
All inputs are finite; a program needn't handle non-finite values.
Results may differ from a plain program's by a relative error of at most 0.02.
The roundings to bfloat16 on the way count: a program that leaves them out, or rounds other values in their place, can miss the bound.
Values may be sent and summed in bfloat16 or wider, within the bound.
No kernel may reach another device: no remote copies, remote signals or barrier semaphores. Data moves between devices by JAX's collectives and lax.ppermute only.
A program may use at most 128 MiB of HBM per device.

v0:
```python
import functools
from types import SimpleNamespace

import jax
import jax.numpy as jnp
from jax import lax
from jax.experimental import pallas as pl
from jax.experimental.pallas import tpu as pltpu
from jax.sharding import PartitionSpec as P

EPSILON = 1e-06
F32 = jnp.float32
BF16 = jnp.bfloat16
EXACT = lax.Precision.HIGHEST
GELU_A = 0.7978845608028654
GELU_B = 0.044715
LANES = 128
HALF = LANES // 2
VMEM_BYTES = 62 * 2**20
HBM = pltpu.HBM
VMEM = pltpu.VMEM
SMEM = pltpu.SMEM


def dot(a, b, ca=1, cb=0, precision=None):
    return lax.dot_general(
        a, b, (((ca,), (cb,)), ((), ())), preferred_element_type=F32, precision=precision
    )


def iota(shape, dim):
    return lax.broadcasted_iota(jnp.int32, shape, dim)


def rms(values):
    return lax.rsqrt(jnp.mean(values * values, axis=-1, keepdims=True) + EPSILON)


def gelu_pair(v):
    square = v * v
    w = 1.0 + jnp.tanh(v * (GELU_A + (GELU_A * GELU_B) * square))
    half = 0.5 * v
    slope = w * (0.5 + half * (2.0 - w) * (GELU_A + (3.0 * GELU_A * GELU_B) * square))
    return half * w, slope


def hot(left, right):
    return (left == right).astype(F32)


class Mover:
    def __init__(self, sems):
        self.sems = sems
        self.used = 0

    def start(self, src, dst):
        copy = pltpu.make_async_copy(src, dst, self.sems.at[self.used])
        self.used += 1
        copy.start()
        return copy


def call(name, body, ins, outs, scratch, sems, cost_us=None):
    names = [n for n, _, _ in ins] + [n for n, _, _, _ in outs] + list(scratch) + ["sems"]

    def kernel(*refs):
        body(SimpleNamespace(**dict(zip(names, refs))))

    results = pl.pallas_call(
        kernel,
        out_shape=[jax.ShapeDtypeStruct(shape, dtype) for _, shape, dtype, _ in outs],
        in_specs=[pl.BlockSpec(memory_space=space) for _, _, space in ins],
        out_specs=[pl.BlockSpec(memory_space=space) for _, _, _, space in outs],
        scratch_shapes=[pltpu.VMEM(shape, dtype) for shape, dtype in scratch.values()]
        + [pltpu.SemaphoreType.DMA((max(sems, 1),))],
        compiler_params=pltpu.CompilerParams(vmem_limit_bytes=VMEM_BYTES),
        cost_estimate=None
        if cost_us is None
        else pl.CostEstimate(flops=int(cost_us * 1e9), bytes_accessed=0, transcendentals=0),
        name=name,
    )(*[array for _, array, _ in ins])
    return SimpleNamespace(**dict(zip([o[0] for o in outs], results)))


def factor_rows(fac_ref, transposed):
    kron = fac_ref.shape[0]
    pieces = [fac_ref[i].T if transposed else fac_ref[i] for i in range(kron)]
    return jnp.concatenate(pieces, axis=0)


class Kron:
    def __init__(self, fac_ref, transposed, left_ref, right_ref):
        kron = left_ref.shape[0]
        self.block = left_ref.shape[1]
        self.inner = right_ref.shape[1]
        self.kron = kron
        width = kron * self.block
        rows = kron * kron
        inner = self.inner
        self.expand = hot(iota((rows, kron), 0) // kron, iota((rows, kron), 1))
        take_c = hot(iota((kron, LANES), 0), iota((kron, LANES), 1) // inner)
        lane_d = iota((inner, LANES), 1)
        take_d = jnp.where(
            lane_d < kron * inner, hot(iota((inner, LANES), 0), lane_d % inner), 0.0
        )
        self.same_a = hot(iota((rows, width), 0) % kron, iota((rows, width), 1) // self.block)
        wide_left = jnp.concatenate([left_ref[...]] * kron, axis=1)
        self.left = dot(self.expand, wide_left, precision=EXACT) * self.same_a
        self.fac = dot(factor_rows(fac_ref, transposed), take_c, precision=EXACT)
        self.right = dot(
            self.expand, dot(right_ref[...], take_d, precision=EXACT), precision=EXACT
        )

    def matrix(self):
        return dot(self.left, self.fac * self.right, 0, 0, precision=EXACT)


class KronBack:
    def __init__(self, kron, block, inner, left, fac, right):
        self.kron, self.block, self.inner = kron, block, inner
        self.left, self.fac, self.right = left, fac, right

    def place(self, of_lane, start):
        lane_in = iota((LANES, LANES), 0)
        keep = (lane_in < self.kron * self.inner) & (iota((LANES, LANES), 1) - start == of_lane(lane_in))
        return keep.astype(BF16)

    def back(self, grad, fac_at, right_at):
        grad = grad.astype(BF16)
        rows = self.kron * self.kron
        width = self.kron * self.block
        inner = dot(self.left.astype(BF16), grad)
        g_fac = dot((inner * self.right).astype(BF16), self.place(lambda n: n // self.inner, fac_at))
        expand = (iota((rows, self.kron), 0) // self.kron == iota((rows, self.kron), 1)).astype(BF16)
        same_i = dot(expand, (inner * self.fac).astype(BF16), 0, 0)
        g_right = dot(same_i.astype(BF16), self.place(lambda n: n % self.inner, right_at))
        outer = dot((self.fac * self.right).astype(BF16), grad, 1, 1)
        outer = outer * hot(iota((rows, width), 0) % self.kron, iota((rows, width), 1) // self.block)
        outer = dot(expand, outer.astype(BF16), 0, 0)
        g_left = sum(outer[:, n * self.block : (n + 1) * self.block] for n in range(self.kron))
        return g_fac, g_right, g_left


def my_mp():
    return lax.axis_index("mp")


def worked(mp):
    return jnp.where(mp < 2, 0, 2)


def gain_row(ref):
    return ref[...].astype(F32).reshape(1, ref.shape[0])


def slot_positions(mp):
    return (mp, mp ^ 2, mp ^ 1, mp ^ 3)


def pick_body(r):
    w = worked(my_mp())
    mover = Mover(r.sems)
    copies = [
        mover.start(r.x.at[2 - w], r.xf),
        mover.start(r.x.at[1], r.xc),
        mover.start(r.t.at[2 - w], r.tf),
    ]
    for copy in copies:
        copy.wait()


def normed(rows, gain):
    values = rows.astype(F32)
    return (values * rms(values) * gain).astype(BF16)


def prep_body(r):
    w = worked(my_mp())
    blk = r.x.shape[1]
    mover = Mover(r.sems)
    copies = [
        mover.start(src, dst)
        for src, dst in (
            (r.x.at[w], r.rows.at[0:blk]),
            (r.x.at[1], r.rows.at[2 * blk : 3 * blk]),
            (r.m1.at[w], r.rows.at[blk : 2 * blk]),
            (r.m1.at[1], r.rows.at[3 * blk : 4 * blk]),
            (r.wk_hbm, r.wk),
            (r.wv_hbm, r.wv),
            (r.wq_hbm, r.wq),
        )
    ]
    down = Kron(r.fac_in, False, r.dl, r.dr)
    up = Kron(r.fac_in, True, r.ur, r.ul)
    for n, one in enumerate((down, up)):
        r.low[n] = one.matrix().astype(BF16)
        r.left[n] = one.left
        r.fac[n] = one.fac
        r.right[n] = one.right
    gain = gain_row(r.gain1)
    for copy in copies[:4]:
        copy.wait()
    for n in range(4):
        rows = slice(n * blk, (n + 1) * blk)
        r.xn[rows] = normed(r.rows[rows], gain)
    copies[4].wait()
    r.k[...] = dot(r.xn[...], r.wk[...]).astype(BF16)
    copies[5].wait()
    r.v[...] = dot(r.xn[...], r.wv[...]).astype(BF16)
    copies[6].wait()
    r.q[0:blk] = dot(r.xn[0:blk], r.wq[...]).astype(BF16)
    r.q[blk : 2 * blk] = dot(r.xn[2 * blk : 3 * blk], r.wq[...]).astype(BF16)


def start_edges(r, mover, seq):
    return [
        mover.start(r.bucket.at[row : row + 8], r.edge.at[n]) for n, row in enumerate((0, seq - 8))
    ]


def bucket_hots(r, seq):
    by_lane = jnp.concatenate([pltpu.roll(r.edge[1, 7:8, :], 1, 1), r.edge[0, 0:1, :]], axis=1)
    return hot(iota((r.table.shape[1], 2 * seq), 0), by_lane)


def fill_bias(r, buckets, blk):
    span = buckets.shape[1]
    by_distance = dot(r.table[...], buckets, precision=EXACT)
    for h in range(by_distance.shape[0]):
        row = by_distance[h : h + 1]
        near = pltpu.roll(
            jnp.broadcast_to(row[:, 2 * blk : 6 * blk], (blk, span // 2)),
            3 * blk,
            1,
            stride=1,
            stride_axis=0,
        )
        r.bias[h, :, 0 : 2 * blk] = jnp.broadcast_to(row[:, 1:2], (blk, 2 * blk))
        r.bias[h, :, 2 * blk : 5 * blk] = near[:, 0 : 3 * blk]
        r.bias[h, :, 5 * blk : 7 * blk] = jnp.broadcast_to(row[:, span - 1 : span], (blk, 2 * blk))


def key_masks(slots, length, blk):
    lane = iota((1, blk), 1)
    return [jnp.where(s * blk + lane < length, 0.0, -jnp.inf).astype(F32) for s in slots]


def by_head(rows):
    half = iota(rows.shape, 1) < HALF
    zero = jnp.zeros_like(rows)
    return jnp.concatenate([jnp.where(half, rows, zero), jnp.where(half, zero, rows)], axis=0)


def attend(hp, q, k, v, bias, mask, slots, q_poss, p, inv_out, ctx_out):
    count = len(q_poss)
    blk = q.shape[0] // count
    low_half = iota((blk, LANES), 1) < HALF
    scores = dot(by_head(q[...]), k[...], 1, 1)
    for u in range(2 * count):
        h, b = divmod(u, count)
        rows = slice(u * blk, (u + 1) * blk)
        parts = []
        for n in range(4):
            place = pl.ds(pl.multiple_of((slots[n] - q_poss[b] + 3) * blk, blk), blk)
            parts.append(
                scores[rows, n * blk : (n + 1) * blk] + (bias[2 * hp + h, :, place] + mask[n])
            )
        top = jnp.max(
            jnp.maximum(jnp.maximum(parts[0], parts[1]), jnp.maximum(parts[2], parts[3])),
            axis=-1,
            keepdims=True,
        )
        parts = [jnp.exp(part - top) for part in parts]
        for n in range(4):
            p[rows, n * blk : (n + 1) * blk] = parts[n].astype(BF16)
    values = v[...]
    out = dot(p[...], jnp.concatenate([values, jnp.ones_like(values)], axis=1))
    inv_all = 1.0 / out[:, LANES:]
    out = out[:, 0:LANES]
    for b in range(count):
        rows = slice(b * blk, (b + 1) * blk)
        inv = jnp.where(
            low_half, inv_all[rows], inv_all[(count + b) * blk : (count + b + 1) * blk]
        )
        inv_out[rows] = inv
        mixed = jnp.where(
            low_half, out[rows], out[(count + b) * blk : (count + b + 1) * blk]
        )
        ctx_out[rows] = (mixed * inv).astype(BF16)


def attend_back(q, k, v, p, do, inv, ctx, count, dq_out, dkt_out, dvt_out):
    blk = q.shape[0] // count
    low_half = iota((blk, LANES), 1) < HALF
    do = by_head(do[...].astype(F32) * inv[...])
    ctx = ctx[...].astype(F32)
    delta = jnp.sum(do * jnp.concatenate([ctx, ctx], axis=0), axis=-1, keepdims=True)
    do = do.astype(BF16)
    dp = dot(do, v[...], 1, 1)
    ds = p[...].astype(F32) * (dp - delta)
    low = ds.astype(BF16)
    dq = dot(low, k[...])
    for b in range(count):
        rows = slice(b * blk, (b + 1) * blk)
        dq_out[rows] = jnp.where(
            low_half, dq[rows], dq[(count + b) * blk : (count + b + 1) * blk]
        ).astype(BF16)
    dkt_out[...] = dot(by_head(q[...]), low, 0, 0).astype(BF16)
    dvt_out[...] = dot(do, p[...], 0, 0).astype(BF16)
    return ds


def main_body(r):
    mp = my_mp()
    w = worked(mp)
    slots = slot_positions(mp)
    blk, width = r.wf.shape
    seq = 4 * blk
    heads = r.table.shape[0]
    pairs = width // LANES
    ffw = r.win.shape[1]
    at = lambda n: slice(n * blk, (n + 1) * blk)
    mover = Mover(r.sems)
    go = lambda pairs_of: [mover.start(src, dst) for src, dst in pairs_of]
    edges = start_edges(r, mover, seq)
    far_rows = go(
        (
            (r.wf, r.rows.at[at(1)]),
            (r.mf, r.rows.at[at(3)]),
            (r.cx, r.rows.at[at(5)]),
            (r.mc, r.rows.at[at(7)]),
        )
    )
    weights_kv = go(((r.wk_hbm, r.wk), (r.wv_hbm, r.wv), (r.wq_hbm, r.wq)))
    shared = go(
        (
            (r.q0.at[at(0)], r.q_s.at[at(0)]),
            (r.k0.at[at(0)], r.k_s.at[at(0)]),
            (r.v0.at[at(0)], r.v_s.at[at(0)]),
            (r.k0.at[at(1)], r.k_s.at[at(2)]),
            (r.v0.at[at(1)], r.v_s.at[at(2)]),
            (r.q0.at[at(1)], r.q_s.at[at(2)]),
            (r.k0.at[at(2)], r.k_s.at[at(4)]),
            (r.v0.at[at(2)], r.v_s.at[at(4)]),
            (r.k0.at[at(3)], r.k_s.at[at(6)]),
            (r.v0.at[at(3)], r.v_s.at[at(6)]),
        )
    )
    gain1 = gain_row(r.gain1)
    gain2 = gain_row(r.gain2)

    for copy in edges:
        copy.wait()
    buckets = bucket_hots(r, seq)
    fill_bias(r, buckets, blk)
    for n in range(4):
        far_rows[n].wait()
        r.far[at(n)] = normed(r.rows[at(2 * n + 1)], gain1)
    for copy, weight, dst in ((weights_kv[0], r.wk, r.k_s), (weights_kv[1], r.wv, r.v_s)):
        copy.wait()
        every = dot(r.far[...], weight[...]).astype(BF16)
        for n in range(4):
            dst[at(2 * n + 1)] = every[at(n)]
    own_rows = go(((r.x.at[w], r.rows.at[at(0)]), (r.x.at[1], r.rows.at[at(4)])))
    weight_o = mover.start(r.wo_hbm, r.wo)
    weight_in = mover.start(r.win_hbm, r.win)
    weight_out = mover.start(r.wout_hbm, r.wout)
    goals = go(
        (
            (r.t.at[w], r.goal.at[at(0)]),
            (r.tf, r.goal.at[at(1)]),
            (r.t.at[1], r.goal.at[at(2)]),
        )
    )
    late = go(
        (
            (r.m1.at[w], r.rows.at[at(2)]),
            (r.m1.at[1], r.rows.at[at(6)]),
        )
    )
    weights_kv[2].wait()
    r.q_s[at(1)] = dot(r.far[at(0)], r.wq[...]).astype(BF16)
    for copy in shared:
        copy.wait()
    masks = [key_masks(slots, r.lengths[n], blk) for n in (w, 1)]
    groups = (
        (slice(0, 2 * blk), (mp, mp ^ 2), slice(0, seq), r.pw_s),
        (at(2), (mp,), slice(seq, 2 * seq), r.pc_s),
    )
    for hp in range(pairs):
        cols = slice(hp * LANES, (hp + 1) * LANES)
        for (q_rows, q_poss, k_rows, p), mask in zip(groups, masks):
            attend(
                hp,
                r.q_s.at[q_rows, cols],
                r.k_s.at[k_rows, cols],
                r.v_s.at[k_rows, cols],
                r.bias,
                mask,
                slots,
                q_poss,
                p.at[hp],
                r.inv_s.at[q_rows, cols],
                r.ctx_s.at[q_rows, cols],
            )

    acc = r.bias
    acc[...] = jnp.zeros_like(acc)

    tokens = 3 * blk
    for copy in own_rows:
        copy.wait()
    own = jnp.concatenate([r.rows[0 : 2 * blk], r.rows[at(4)]], axis=0).astype(F32)
    weight_o.wait()
    residual = own + dot(r.ctx_s[...], r.wo[...])
    r.res[...] = residual
    inv2 = rms(residual)
    r.xn[...] = (residual * inv2 * gain2).astype(BF16)
    weight_in.wait()
    weight_out.wait()
    chunk = 512
    chunks = [slice(n * chunk, (n + 1) * chunk) for n in range(ffw // chunk)]
    pre = dot(r.xn[...], r.win[:, chunks[0]])
    total = None
    for n, cols in enumerate(chunks):
        ahead = dot(r.xn[...], r.win[:, chunks[n + 1]]) if n + 1 < len(chunks) else None
        value, slope = gelu_pair(pre)
        value = value.astype(BF16)
        r.slope[:, cols] = slope.astype(BF16)
        part = dot(value, r.wout[cols, :])
        total = part if total is None else total + part
        pre = ahead
    r.ffn[...] = total.astype(BF16)

    down_low = r.low[0]
    up_low = r.low[1]
    ffn = r.ffn[...]
    activated, act_slope = gelu_pair(dot(ffn, down_low))
    activated = activated.astype(BF16)
    final = r.res[...] + ffn.astype(F32) + dot(activated, up_low, 1, 1)
    r.blk_s[...] = final.astype(BF16)
    out = go(
        (
            (r.blk_s.at[at(1)], r.blk_f),
            (r.blk_s.at[at(0)], r.blk_own.at[0]),
            (r.blk_s.at[at(2)], r.blk_own.at[1]),
        )
    )
    row = iota((blk, 1), 0)
    valid = jnp.concatenate(
        [
            pos * blk + row < length
            for pos, length in ((mp, r.lengths[w]), (mp ^ 2, r.lengths[w]), (mp, r.lengths[1]))
        ],
        axis=0,
    )
    for copy in goals:
        copy.wait()
    err = jnp.where(valid, final - r.goal[...].astype(F32), 0.0)
    r.err[...] = err
    loss = 0.5 * jnp.sum(jnp.sum(err * err, axis=0, keepdims=True), axis=1, keepdims=True)
    g_adapter = err.astype(BF16)
    grad_up = dot(g_adapter, activated, 0, 0)
    g_squeezed = (dot(g_adapter, up_low) * act_slope).astype(BF16)
    grad_down = dot(ffn, g_squeezed, 0, 0)
    kron, block, inner = r.shape_kron
    backs = [
        KronBack(kron, block, inner, r.left[n], r.fac[n], r.right[n]).back(grad, *PACK_KRON[n])
        for n, grad in enumerate((grad_down, grad_up))
    ]
    r.ffn[...] = (err + dot(g_squeezed, down_low, 1, 1)).astype(BF16)

    for n in range(ffw // chunk):
        cols = slice(n * chunk, (n + 1) * chunk)
        r.hid[:, cols] = (dot(r.ffn[...], r.wout[cols, :], 1, 1) * r.slope[:, cols].astype(F32)).astype(
            BF16
        )
    g_normed = jnp.concatenate(
        [dot(r.hid[...], r.win[n * 256 : (n + 1) * 256, :], 1, 1) for n in range(width // 256)],
        axis=1,
    )
    residual = r.res[...]
    inv2 = rms(residual)
    g2 = jnp.sum(g_normed * residual * inv2, axis=0, keepdims=True)
    weighted = g_normed * gain2
    mean = jnp.mean(weighted * residual, axis=-1, keepdims=True)
    g_res = r.err[...] + inv2 * weighted - residual * (inv2 * inv2 * inv2 * mean)
    r.err[...] = g_res
    r.do[...] = dot(g_res.astype(BF16), r.wo[...], 1, 1).astype(BF16)

    for hp in range(pairs):
        cols = slice(hp * LANES, (hp + 1) * LANES)
        scores = []
        for q_rows, q_poss, k_rows, p in groups:
            scores.append(
                attend_back(
                    r.q_s.at[q_rows, cols],
                    r.k_s.at[k_rows, cols],
                    r.v_s.at[k_rows, cols],
                    p.at[hp],
                    r.do.at[q_rows, cols],
                    r.inv_s.at[q_rows, cols],
                    r.ctx_s.at[q_rows, cols],
                    len(q_poss),
                    r.dq.at[q_rows, cols],
                    r.dkt.at[cols, k_rows],
                    r.dvt.at[cols, k_rows],
                )
            )
        for h in range(2):
            near = scores[0][2 * h * blk : (2 * h + 1) * blk] + scores[1][h * blk : (h + 1) * blk]
            far = scores[0][(2 * h + 1) * blk : (2 * h + 2) * blk]
            for piece, q_pos in ((near, mp), (far, mp ^ 2)):
                for n in range(4):
                    place = pl.ds(pl.multiple_of((slots[n] - q_pos + 3) * blk, blk), blk)
                    acc[2 * hp + h, :, place] += piece[:, n * blk : (n + 1) * blk]

    sub = iota((8, seq), 0)

    def along_diagonals(h):
        total = jnp.zeros((8, seq), F32)
        for g in range(blk // 8):
            near = jnp.concatenate(
                [acc[h, 8 * g : 8 * g + 8, 2 * blk : 5 * blk], jnp.zeros((8, blk), F32)], axis=1
            )
            total = total + pltpu.roll(near, blk - 8 * g, 1)
        for bit in (1, 2, 4):
            total = jnp.where((sub & bit) > 0, pltpu.roll(total, seq - bit, 1), total)
        near = jnp.sum(total, axis=0, keepdims=True)
        below = jnp.sum(acc[h, :, 0 : 2 * blk], axis=0, keepdims=True)
        above = jnp.sum(acc[h, :, 5 * blk : 7 * blk], axis=0, keepdims=True)
        return jnp.concatenate(
            [
                jnp.zeros((1, blk), F32),
                below[:, 0:blk],
                below[:, blk : 2 * blk] + near[:, 0:blk],
                near[:, blk:seq],
                above,
            ],
            axis=1,
        )

    for copy in late:
        copy.wait()
    sums = []
    g1 = jnp.zeros((1, width), F32)
    side = 256
    for first, dq_rows in ((0, slice(0, 2 * blk)), (4, at(2))):
        cols = slice(first * blk, first * blk + seq)
        pieces = []
        for n in range(width // side):
            outs = slice(n * side, (n + 1) * side)
            piece = dot(r.dkt[:, cols], r.wk[outs, :], 0, 1)
            if len(sums) < heads:
                sums.append(along_diagonals(len(sums)))
            piece = piece + dot(r.dvt[:, cols], r.wv[outs, :], 0, 1)
            if len(sums) < heads:
                sums.append(along_diagonals(len(sums)))
            pieces.append(piece)
        parts = jnp.concatenate(pieces, axis=1)
        own = dot(r.dq[dq_rows], r.wq[...], 1, 1)
        for n in range(4):
            part = parts[at(n)]
            if n * blk < own.shape[0]:
                part = part + own[at(n)]
            values = r.rows[at(first + n)].astype(F32)
            inv1 = rms(values)
            scaled = part * values
            g1 = g1 + jnp.sum(scaled * inv1, axis=0, keepdims=True)
            mean = jnp.mean(scaled * gain1, axis=-1, keepdims=True)
            back = inv1 * (part * gain1) - values * (inv1 * inv1 * inv1 * mean)
            if n < 2:
                m = n if first == 0 else 2 + n
                if m < 3:
                    back = back + r.err[at(m)]
                r.base_s[at(m)] = back
                out += go(((r.base_s.at[at(m)], r.base.at[m]),))
            else:
                m = n - 2 if first == 0 else n
                r.send_s[at(m)] = back.astype(BF16)
                out += go(((r.send_s.at[at(m)], r.send.at[m]),))
    for h in range(len(sums), heads):
        sums.append(along_diagonals(h))
    g_table = dot(jnp.concatenate(sums, axis=0), buckets, 1, 1, precision=EXACT)

    (gf_d, g_dr, g_dl), (gf_u, g_ul, g_ur) = backs
    row16 = iota((16, LANES), 0)
    lane16 = iota((16, LANES), 1)
    pack = r.pack
    pack[0:16] = gf_d + gf_u
    pack[0:4] += g_dr + g_ul
    pack[0:heads, 0 : r.table.shape[1]] = g_table
    pack[0:4, HALF:LANES] = g_dl[:, 0:HALF]
    pack[4:8, HALF:LANES] = g_dl[:, HALF : 2 * HALF]
    pack[8:12, HALF:LANES] = g_dl[:, 2 * HALF : 3 * HALF]
    pack[12:16, HALF:LANES] = g_ur[:, 0:HALF]
    pack[16:20] = g_ur[:, HALF : 3 * HALF]
    for n in range(width // LANES):
        pack[20 + n : 21 + n] = g1[:, n * LANES : (n + 1) * LANES]
        pack[26 + n : 27 + n] = g2[:, n * LANES : (n + 1) * LANES]
    real = (r.lengths[0] + r.lengths[1] + r.lengths[2]).astype(F32)
    both = jnp.where(lane16 < 2, loss, real)
    high = both.astype(BF16).astype(F32)
    both = jnp.where(lane16 % 2 == 0, high, both - high)
    r.small[0:16] = jnp.where((row16 == 15) & (lane16 < 4), both, pack[0:16]).astype(BF16)
    r.small[16:32] = pack[16:32].astype(BF16)
    for copy in out:
        copy.wait()


PACK_KRON = ((32, 40), (36, 52))


def middle_body(r):
    mover = Mover(r.sems)
    copies = [
        mover.start(src, dst)
        for src, dst in (
            (r.base.at[1], r.base_s.at[0]),
            (r.recv.at[1], r.recv_s.at[0]),
            (r.base.at[3], r.base_s.at[1]),
            (r.recv.at[3], r.recv_s.at[1]),
            (r.blk_f, r.away.at[2]),
        )
    ]
    spread = r.small.shape[0] // 2
    first = pl.multiple_of((my_mp() % 2) * spread, spread)
    half = r.small[pl.ds(first, spread)].astype(F32) + r.others[pl.ds(first, spread)].astype(F32)
    row = iota(half.shape, 0)
    lane = iota(half.shape, 1)
    even = lane % 2 == 0
    whole = half + jnp.where(even, pltpu.roll(half, LANES - 1, 1), pltpu.roll(half, 1, 1))
    high = whole.astype(BF16).astype(F32)
    parted = (row == 15) & (lane < 4) & (my_mp() % 2 == 0)
    half = jnp.where(parted, jnp.where(even, high, whole - high), half).astype(BF16)
    for n in range(r.spread.shape[0]):
        r.spread[n] = half
    for n in range(2):
        copies[2 * n].wait()
        copies[2 * n + 1].wait()
        r.away[n] = (r.base_s[n] + r.recv_s[n].astype(F32)).astype(BF16)
    copies[4].wait()


def finish_body(token_total, seq_total, r):
    w = worked(my_mp())
    width = r.grad.shape[2]
    mover = Mover(r.sems)
    copies = [
        mover.start(src, dst)
        for src, dst in (
            (r.gathered, r.gathered_s),
            (r.back.at[0], r.back_s.at[0]),
            (r.back.at[1], r.back_s.at[1]),
            (r.base.at[0], r.base_s.at[0]),
            (r.recv.at[0], r.recv_s.at[0]),
            (r.base.at[2], r.base_s.at[1]),
            (r.recv.at[2], r.recv_s.at[1]),
            (r.back.at[2], r.block.at[2 - w]),
            (r.blk_own.at[0], r.block.at[w]),
            (r.blk_own.at[1], r.block.at[1]),
        )
    ]
    copies[0].wait()
    halves = [r.gathered_s[n].astype(F32) for n in range(2)]
    for n in range(2, r.gathered_s.shape[0]):
        halves[n % 2] = halves[n % 2] + r.gathered_s[n].astype(F32)
    total = jnp.concatenate(halves, axis=0)
    tail = total[15:16, 0:4]
    count = (tail[:, 2:3] + tail[:, 3:4]) * 0.25
    scale = token_total / count
    params = [r.dl, r.dr, r.ul, r.ur]
    squares = [jnp.sum(r.fac[n] * r.fac[n], keepdims=True) for n in range(r.fac.shape[0])]
    squares += [jnp.sum(p[...] * p[...], keepdims=True) for p in params]
    penalty = 0.5 * seq_total * sum(squares)
    r.loss[...] = (scale * (tail[:, 0:1] + tail[:, 1:2]) + penalty) / (token_total * width)

    heads, buckets = r.g_table.shape
    r.g_table[...] = scale * total[0:heads, 0:buckets]
    kron = r.fac.shape[0]
    for i in range(kron):
        rows = slice(i * kron, (i + 1) * kron)
        r.g_fac[i] = (
            scale * (total[rows, 32 : 32 + kron] + total[rows, 36 : 36 + kron].T)
            + seq_total * r.fac[i]
        )
    r.g_dr[...] = scale * total[0:4, 40:52] + seq_total * r.dr[...]
    r.g_ul[...] = scale * total[0:4, 52:64] + seq_total * r.ul[...]
    g_dl = jnp.concatenate([total[4 * n : 4 * n + 4, HALF:LANES] for n in range(3)], axis=1)
    r.g_dl[...] = scale * g_dl + seq_total * r.dl[...]
    g_ur = jnp.concatenate([total[12:16, HALF:LANES], total[16:20]], axis=1)
    r.g_ur[...] = scale * g_ur + seq_total * r.ur[...]
    for n in range(width // LANES):
        r.g1[n : n + 1] = scale * total[20 + n : 21 + n]
        r.g2[n : n + 1] = scale * total[26 + n : 27 + n]

    for copy in copies[1:]:
        copy.wait()
    r.grad[2 - w] = scale * r.back_s[0].astype(F32)
    r.grad[w] = scale * (r.base_s[0] + r.recv_s[0].astype(F32))
    r.grad[1] = scale * (r.base_s[1] + r.recv_s[1].astype(F32) + r.back_s[1].astype(F32))


def local(
    layer_input,
    targets,
    attn_gain,
    ffn_gain,
    query_matrix,
    key_matrix,
    value_matrix,
    attention_output_weight,
    feedforward_input_weight,
    feedforward_output_weight,
    bias_table,
    factors,
    down_left,
    down_right,
    up_left,
    up_right,
    lengths,
    relative_bucket,
):
    seqs, blk, width = layer_input.shape
    mp_size = lax.axis_size("mp")
    axes = ("dp", "mp")
    devices = lax.axis_size("dp") * mp_size
    heads = bias_table.shape[1]
    ffw = feedforward_input_weight.shape[1]
    kron = factors.shape[0]
    seq_total = lax.axis_size("dp") * seqs
    token_total = seq_total * blk * mp_size
    assert seqs == 3 and mp_size == 4
    core = [(i, i ^ 1) for i in range(mp_size)]
    chip = [(i, i ^ 2) for i in range(mp_size)]
    pairs = heads // 2
    seq = blk * mp_size
    table = bias_table.T
    square = ((width, width), BF16)
    rows = lambda n, dtype=BF16: ((n * blk, width), dtype)

    picked = call(
        "pick",
        pick_body,
        [("x", layer_input, HBM), ("t", targets, HBM)],
        [(n, (blk, width), BF16, VMEM) for n in ("xf", "xc", "tf")],
        {},
        3,
    )
    wf = lax.ppermute(picked.xf, "mp", chip)
    cx = lax.ppermute(picked.xc, "mp", chip)
    tf = lax.ppermute(picked.tf, "mp", chip)
    m1 = lax.ppermute(layer_input, "mp", core)
    prep = call(
        "prep",
        prep_body,
        [
            ("x", layer_input, HBM),
            ("m1", m1, HBM),
            ("gain1", attn_gain, VMEM),
            ("fac_in", factors, VMEM),
            ("dl", down_left, VMEM),
            ("dr", down_right, VMEM),
            ("ul", up_left, VMEM),
            ("ur", up_right, VMEM),
            ("wq_hbm", query_matrix, HBM),
            ("wk_hbm", key_matrix, HBM),
            ("wv_hbm", value_matrix, HBM),
        ],
        [
            ("q",) + rows(2) + (VMEM,),
            ("k",) + rows(4) + (VMEM,),
            ("v",) + rows(4) + (VMEM,),
            ("low", (2, width, LANES), BF16, VMEM),
            ("left", (2, kron * kron, width), F32, VMEM),
            ("fac", (2, kron * kron, LANES), F32, VMEM),
            ("right", (2, kron * kron, LANES), F32, VMEM),
        ],
        {"rows": rows(4), "xn": rows(4), "wq": square, "wk": square, "wv": square},
        7,
        4.0,
    )

    wf, cx, prep.k = lax.optimization_barrier((wf, cx, prep.k))
    mf = lax.ppermute(wf, "mp", core)
    mc = lax.ppermute(cx, "mp", core)

    def main_with_shape(r):
        r.shape_kron = (kron, down_left.shape[1], down_right.shape[1])
        main_body(r)

    main = call(
        "main",
        main_with_shape,
        [
            ("lengths", lengths, SMEM),
            ("x", layer_input, HBM),
            ("t", targets, HBM),
            ("wf", wf, HBM),
            ("cx", cx, HBM),
            ("tf", tf, HBM),
            ("m1", m1, HBM),
            ("mf", mf, HBM),
            ("mc", mc, HBM),
            ("gain1", attn_gain, VMEM),
            ("gain2", ffn_gain, VMEM),
            ("table", table, VMEM),
            ("bucket", relative_bucket, HBM),
            ("low", prep.low, VMEM),
            ("left", prep.left, VMEM),
            ("fac", prep.fac, VMEM),
            ("right", prep.right, VMEM),
            ("q0", prep.q, HBM),
            ("k0", prep.k, HBM),
            ("v0", prep.v, HBM),
            ("wq_hbm", query_matrix, HBM),
            ("wk_hbm", key_matrix, HBM),
            ("wv_hbm", value_matrix, HBM),
            ("wo_hbm", attention_output_weight, HBM),
            ("win_hbm", feedforward_input_weight, HBM),
            ("wout_hbm", feedforward_output_weight, HBM),
        ],
        [
            ("blk_own", (2, blk, width), BF16, HBM),
            ("blk_f", (blk, width), BF16, HBM),
            ("base", (4, blk, width), F32, HBM),
            ("send", (4, blk, width), BF16, HBM),
            ("small", (32, LANES), BF16, VMEM),
        ],
        {
            "wq": square,
            "wk": square,
            "wv": square,
            "wo": square,
            "win": ((width, ffw), BF16),
            "wout": ((ffw, width), BF16),
            "edge": ((2, 8, seq), jnp.int32),
            "rows": rows(8),
            "goal": rows(3),
            "xn": rows(3),
            "q_s": rows(3),
            "k_s": rows(8),
            "v_s": rows(8),
            "far": rows(4),
            "bias": ((heads, blk, 7 * blk), F32),
            "pack": ((32, LANES), F32),
            "pw_s": ((pairs, seq, seq), BF16),
            "pc_s": ((pairs, 2 * blk, seq), BF16),
            "ctx_s": rows(3),
            "inv_s": rows(3, F32),
            "res": rows(3, F32),
            "hid": ((3 * blk, ffw), BF16),
            "slope": ((3 * blk, ffw), BF16),
            "ffn": rows(3),
            "err": rows(3, F32),
            "do": rows(3),
            "dq": rows(3),
            "dkt": ((width, 2 * seq), BF16),
            "dvt": ((width, 2 * seq), BF16),
            "blk_s": rows(3),
            "base_s": rows(4, F32),
            "send_s": rows(4),
        },
        44,
        28.0,
    )
    recv = lax.ppermute(main.send, "mp", core)
    others = lax.ppermute(main.small, "mp", core)
    pair = lambda dtype: ((2, blk, width), dtype)
    middle = call(
        "middle",
        middle_body,
        [("base", main.base, HBM), ("recv", recv, HBM), ("blk_f", main.blk_f, HBM), ("small", main.small, VMEM), ("others", others, VMEM)],
        [("away", (3, blk, width), BF16, VMEM), ("spread", (devices, 16, LANES), BF16, VMEM)],
        {"base_s": pair(F32), "recv_s": pair(BF16)},
        5,
    )
    spread, away = lax.optimization_barrier((middle.spread, middle.away))
    back = lax.ppermute(away, "mp", chip)
    gathered = lax.all_to_all(spread, axes, split_axis=0, concat_axis=0, tiled=True)

    done = call(
        "finish",
        functools.partial(finish_body, float(token_total), float(seq_total)),
        [
            ("gathered", gathered, HBM),
            ("base", main.base, HBM),
            ("recv", recv, HBM),
            ("back", back, HBM),
            ("blk_own", main.blk_own, HBM),
            ("fac", factors, VMEM),
            ("dl", down_left, VMEM),
            ("dr", down_right, VMEM),
            ("ul", up_left, VMEM),
            ("ur", up_right, VMEM),
        ],
        [
            ("loss", (1, 1), F32, VMEM),
            ("block", (seqs, blk, width), BF16, VMEM),
            ("grad", (seqs, blk, width), F32, VMEM),
            ("g1", (width // LANES, LANES), F32, VMEM),
            ("g2", (width // LANES, LANES), F32, VMEM),
            ("g_table", table.shape, F32, VMEM),
            ("g_fac", factors.shape, F32, VMEM),
            ("g_dl", down_left.shape, F32, VMEM),
            ("g_dr", down_right.shape, F32, VMEM),
            ("g_ul", up_left.shape, F32, VMEM),
            ("g_ur", up_right.shape, F32, VMEM),
        ],
        {
            "gathered_s": ((devices, 16, LANES), BF16),
            "back_s": pair(BF16),
            "base_s": pair(F32),
            "recv_s": pair(BF16),
        },
        10,
    )
    return (
        done.loss.reshape(()),
        done.block,
        done.grad,
        done.g1.reshape(width),
        done.g2.reshape(width),
        done.g_table.T,
        done.g_fac,
        done.g_dl,
        done.g_dr,
        done.g_ul,
        done.g_ur,
    )


def solution(mesh):
    rows = P("dp", "mp", None)
    return jax.shard_map(
        local,
        mesh=mesh,
        in_specs=(rows, rows) + (P(),) * 14 + (P("dp"), P()),
        out_specs=(P(), rows, rows) + (P(),) * 8,
        check_vma=False,
    )
```

profile of v0, /device:TPU:0, one launch (start us, length us, event | category | flops | bytes accessed | tf_op | source)
XLA Modules:
  0.0 87.0 jit_solution(10878253937346351379)
XLA Ops:
  0.6 0.5 collective-permute-start.2
  1.2 2.0 %pick.1 = (bf16[128,768]{1,0:T(8,128)(2,1)}, bf16[128,768]{1,0:T(8,128)(2,1)}, bf16[128,768]{1,0:T(8,128)(2,1)}) custom-call(bf16[3,128,768]{2,1,0:T(8,128)(2,1)} %refs_1_.3, bf16[3,128,768]{2,1,0:T(8,128)(2,1)} %refs_2_.3), custom_call_target="tpu_custom_call" | custom-call | tf_op jit(solution)/shard_map/pick/pallas_call | solution.py:69
  3.2 2.6 %collective-permute-start = (bf16[128,768]{1,0:T(8,128)(2,1)}, bf16[128,768]{1,0:T(8,128)(2,1)S(1)}, u32[]{:S(2)}, u32[]{:S(2)}) collective-permute-start(bf16[128,768]{1,0:T(8,128)(2,1)} %get-tuple-element.44), channel_id=1, source_target_pairs={{0,2},{1,3},{2,0},{3,1},{4,6},{5,7},{6,4},{7,5},{8,10},{9,11},{10,... | collective-permute-start | bytes 589832 | tf_op jit(solution)/shard_map/ppermute | solution.py:750
  5.7 0.1 collective-permute-start.1
  5.8 1.9 %collective-permute-start.3 = (bf16[128,768]{1,0:T(8,128)(2,1)}, bf16[128,768]{1,0:T(8,128)(2,1)S(1)}, u32[]{:S(2)}, u32[]{:S(2)}) collective-permute-start(bf16[128,768]{1,0:T(8,128)(2,1)} %get-tuple-element.49), channel_id=1, source_target_pairs={{0,2},{1,3},{2,0},{3,1},{4,6},{5,7},{6,4},{7,5},{8,10},{9,11},{10,... | collective-permute-start | bytes 589832 | tf_op jit(solution)/shard_map/ppermute | solution.py:752
  7.8 0.0 collective-permute-done.2.refs_1_.refs_6_
  7.8 0.8 copy-done.3
  8.6 6.0 %prep.1 = (bf16[256,768]{1,0:T(8,128)(2,1)}, bf16[512,768]{1,0:T(8,128)(2,1)}, bf16[512,768]{1,0:T(8,128)(2,1)}, bf16[2,768,128]{2,1,0:T(8,128)(2,1)}, f32[2,16,...) custom-call(bf16[3,128,768]{2,1,0:T(8,128)(2,1)} %refs_1_.3, bf16[3,128,768]{2,1,0:T(8,128)(2,1)} %copy-done.3, ...), custom_call_target="tpu_custom_call" | custom-call | flops 4000000000 | tf_op jit(solution)/shard_map/prep/pallas_call | solution.py:69
  14.6 0.0 collective-permute-done.refs_3_
  14.6 0.0 copy-start.4
  14.6 1.3 %collective-permute-done.1.refs_4_ = bf16[128,768]{1,0:T(8,128)(2,1)S(1)} collective-permute-done((bf16[128,768]{1,0:T(8,128)(2,1)}, bf16[128,768]{1,0:T(8,128)(2,1)S(1)}, u32[]{:S(2)}, u32[]{:S(2)}) %collective-permute-start.1) | collective-permute-done | bytes 196640 | tf_op jit(solution)/shard_map/ppermute | solution.py:751
  15.9 0.0 collective-permute-start.4
  15.9 0.5 collective-permute-start.5
  16.4 3.5 %collective-permute-done.3.refs_5_ = bf16[128,768]{1,0:T(8,128)(2,1)S(1)} collective-permute-done((bf16[128,768]{1,0:T(8,128)(2,1)}, bf16[128,768]{1,0:T(8,128)(2,1)S(1)}, u32[]{:S(2)}, u32[]{:S(2)}) %collective-permute-start.3) | collective-permute-done | bytes 196640 | tf_op jit(solution)/shard_map/ppermute | solution.py:752
  19.9 0.0 collective-permute-done.4.refs_7_
  19.9 0.0 collective-permute-done.5.refs_8_
  20.0 0.6 copy-done.6
  20.6 0.1 copy-done.7
  20.7 0.1 copy-done.8
  20.7 36.8 %main.1 = (bf16[2,128,768]{2,1,0:T(8,128)(2,1)}, bf16[128,768]{1,0:T(8,128)(2,1)}, f32[4,128,768]{2,1,0:T(8,128)}, bf16[4,128,768]{2,1,0:T(8,128)(2,1)}, bf16[32,128]{1,0:T(8,128)(2,1)}) custom-call(s32[3]{0:T(128)} %refs_0_.5, bf16[3,128,768]{2,1,0:T(8,128)(2,1)} %refs_1_.3, bf16[3,128,768]{2,1,0:T(8,128)(2,1)} %refs_2_.3, bf16[128,768]{1,0:T(8,128)(2,1)} %copy-done.4, ...), custom_call_target="tpu_custom_call" | custom-call | flops 28000000000 | tf_op jit(solution)/shard_map/main/pallas_call | solution.py:69
  57.5 0.1 collective-permute-start.6
  57.6 0.5 collective-permute-start.7
  58.1 2.0 %collective-permute-done.7.refs_4_ = bf16[32,128]{1,0:T(8,128)(2,1)S(1)} collective-permute-done((bf16[32,128]{1,0:T(8,128)(2,1)}, bf16[32,128]{1,0:T(8,128)(2,1)S(1)}, u32[]{:S(2)}, u32[]{:S(2)}) %collective-permute-start.7) | collective-permute-done | bytes 8224 | tf_op jit(solution)/shard_map/ppermute | solution.py:868
  60.1 0.0 collective-permute-done.6.refs_1_.refs_2_
  60.1 0.6 copy-done.2
  60.7 0.3 copy-done
  61.0 2.9 %middle.1 = (bf16[3,128,768]{2,1,0:T(8,128)(2,1)}, bf16[32,16,128]{2,1,0:T(8,128)(2,1)}) custom-call(f32[4,128,768]{2,1,0:T(8,128)} %get-tuple-element.57.refs_0_.refs_1_, bf16[4,128,768]{2,1,0:T(8,128)(2,1)} %copy-done, bf16[128,768]{1,0:T(8,128)(2,1)} %get-tuple-element.59.refs_2_, bf16[32,128]{1,0:T(8,128)(2,1)} %get-tuple-element.60.refs_3_, ...), custom_call_target="tpu_custom_call" | custom-call | tf_op jit(solution)/shard_map/middle/pallas_call | solution.py:69
  63.9 1.8 %collective-permute-start.8 = (bf16[3,128,768]{2,1,0:T(8,128)(2,1)}, bf16[3,128,768]{2,1,0:T(8,128)(2,1)S(1)}, u32[]{:S(2)}, u32[]{:S(2)}) collective-permute-start(bf16[3,128,768]{2,1,0:T(8,128)(2,1)} %get-tuple-element.64), channel_id=1, source_target_pairs={{0,2},{1,3},{2,0},{3,1},{4,6},{5,7},{6,4},{7,5},{8,10},{9,11},{10,... | collective-permute-start | bytes 1769480 | tf_op jit(solution)/shard_map/ppermute | solution.py:879
  65.7 16.5 %all_to_all.5.refs_0_ = bf16[32,16,128]{2,1,0:T(8,128)(2,1)} all-to-all(bf16[32,16,128]{2,1,0:T(8,128)(2,1)} %get-tuple-element.63), channel_id=1, replica_groups=mesh['dp'=8,'mp'=4] {'dp','mp'}, dimensions={0} | all-to-all | bytes 262144 | tf_op jit(solution)/shard_map/all_to_all | solution.py:880
  82.3 0.0 collective-permute-done.8.refs_3_
  82.3 0.8 copy-done.1
  83.1 3.8 %finish.1 = (f32[1,1]{1,0:T(1,128)}, bf16[3,128,768]{2,1,0:T(8,128)(2,1)}, f32[3,128,768]{2,1,0:T(8,128)}, f32[6,128]{1,0:T(8,128)}, f32[6,128]{1,0:T(8,128)}, /...) custom-call(bf16[32,16,128]{2,1,0:T(8,128)(2,1)} %all_to_all.5.refs_, ...), custom_call_target="tpu_custom_call" | custom-call | tf_op jit(solution)/shard_map/finish/pallas_call | solution.py:69
  (10 shorter events, 0.0 us)
Async XLA Ops:
  0.6 7.1 %collective-permute-start.2 = (bf16[3,128,768]{2,1,0:T(8,128)(2,1)}, bf16[3,128,768]{2,1,0:T(8,128)(2,1)S(1)}, u32[]{:S(2)}, u32[]{:S(2)}) collective-permute-start(bf16[3,128,768]{2,1,0:T(8,128)(2,1)} %refs_1_.3), channel_id=1, source_target_pairs={{0,1},{1,0},{2,3},{3,2},{4,5},{5,4},{6,7},{7,6},{8,9},{9,8},{10,11... | collective-permute-start | bytes 1769480 | tf_op jit(solution)/shard_map/ppermute | solution.py:753
  3.2 11.4 %collective-permute-start = (bf16[128,768]{1,0:T(8,128)(2,1)}, bf16[128,768]{1,0:T(8,128)(2,1)S(1)}, u32[]{:S(2)}, u32[]{:S(2)}) collective-permute-start(bf16[128,768]{1,0:T(8,128)(2,1)} %get-tuple-element.44), channel_id=1, source_target_pairs={{0,2},{1,3},{2,0},{3,1},{4,6},{5,7},{6,4},{7,5},{8,10},{9,11},{10,... | collective-permute-start | bytes 589832 | tf_op jit(solution)/shard_map/ppermute | solution.py:750
  5.7 10.2 %collective-permute-start.1 = (bf16[128,768]{1,0:T(8,128)(2,1)}, bf16[128,768]{1,0:T(8,128)(2,1)S(1)}, u32[]{:S(2)}, u32[]{:S(2)}) collective-permute-start(bf16[128,768]{1,0:T(8,128)(2,1)} %get-tuple-element.45), channel_id=1, source_target_pairs={{0,2},{1,3},{2,0},{3,1},{4,6},{5,7},{6,4},{7,5},{8,10},{9,11},{10,... | collective-permute-start | bytes 589832 | tf_op jit(solution)/shard_map/ppermute | solution.py:751
  5.8 14.1 %collective-permute-start.3 = (bf16[128,768]{1,0:T(8,128)(2,1)}, bf16[128,768]{1,0:T(8,128)(2,1)S(1)}, u32[]{:S(2)}, u32[]{:S(2)}) collective-permute-start(bf16[128,768]{1,0:T(8,128)(2,1)} %get-tuple-element.49), channel_id=1, source_target_pairs={{0,2},{1,3},{2,0},{3,1},{4,6},{5,7},{6,4},{7,5},{8,10},{9,11},{10,... | collective-permute-start | bytes 589832 | tf_op jit(solution)/shard_map/ppermute | solution.py:752
  7.8 0.8 copy-start.3
  14.6 5.4 %copy-start.4 = (bf16[128,768]{1,0:T(8,128)(2,1)}, bf16[128,768]{1,0:T(8,128)(2,1)S(1)}, u32[]{:S(2)}) copy-start(bf16[128,768]{1,0:T(8,128)(2,1)S(1)} %collective-permute-done.refs_3_) | copy-start | bytes 589828
  15.9 4.0 %copy-start.5 = (bf16[128,768]{1,0:T(8,128)(2,1)}, bf16[128,768]{1,0:T(8,128)(2,1)S(1)}, u32[]{:S(2)}) copy-start(bf16[128,768]{1,0:T(8,128)(2,1)S(1)} %collective-permute-done.1.refs_4_) | copy-start | bytes 589828
  15.9 4.0 %collective-permute-start.4 = (bf16[128,768]{1,0:T(8,128)(2,1)S(1)}, bf16[128,768]{1,0:T(8,128)(2,1)S(1)}, u32[]{:S(2)}, u32[]{:S(2)}) collective-permute-start(bf16[128,768]{1,0:T(8,128)(2,1)S(1)} %collective-permute-done.refs_3_), channel_id=1, source_target_pairs={{0,1},{1,0},{2,3},{3,2},{4,5},{5,4},{6,7},{7,6},{8,9},{9,8},{10,11... | collective-permute-start | bytes 589832 | tf_op jit(solution)/shard_map/ppermute | solution.py:785
  15.9 4.0 %collective-permute-start.5 = (bf16[128,768]{1,0:T(8,128)(2,1)S(1)}, bf16[128,768]{1,0:T(8,128)(2,1)S(1)}, u32[]{:S(2)}, u32[]{:S(2)}) collective-permute-start(bf16[128,768]{1,0:T(8,128)(2,1)S(1)} %collective-permute-done.1.refs_4_), channel_id=1, source_target_pairs={{0,1},{1,0},{2,3},{3,2},{4,5},{5,4},{6,7},{7,6},{8,9},{9,8},{10,11... | collective-permute-start | bytes 589832 | tf_op jit(solution)/shard_map/ppermute | solution.py:786
  19.9 0.7 copy-start.6
  19.9 0.8 copy-start.7
  19.9 0.8 copy-start.8
  57.5 2.6 %collective-permute-start.6 = (bf16[4,128,768]{2,1,0:T(8,128)(2,1)}, bf16[4,128,768]{2,1,0:T(8,128)(2,1)S(1)}, u32[]{:S(2)}, u32[]{:S(2)}) collective-permute-start(bf16[4,128,768]{2,1,0:T(8,128)(2,1)} %get-tuple-element.58), channel_id=1, source_target_pairs={{0,1},{1,0},{2,3},{3,2},{4,5},{5,4},{6,7},{7,6},{8,9},{9,8},{10,11... | collective-permute-start | bytes 2359304 | tf_op jit(solution)/shard_map/ppermute | solution.py:867
  57.6 2.5 %collective-permute-start.7 = (bf16[32,128]{1,0:T(8,128)(2,1)}, bf16[32,128]{1,0:T(8,128)(2,1)S(1)}, u32[]{:S(2)}, u32[]{:S(2)}) collective-permute-start(bf16[32,128]{1,0:T(8,128)(2,1)} %get-tuple-element.60.refs_3_), channel_id=1, source_target_pairs={{0,1},{1,0},{2,3},{3,2},{4,5},{5,4},{6,7},{7,6},{8,9},{9,8},{10,11... | collective-permute-start | bytes 24584 | tf_op jit(solution)/shard_map/ppermute | solution.py:868
  60.1 0.6 copy-start.2
  60.1 0.9 %copy-start = (bf16[4,128,768]{2,1,0:T(8,128)(2,1)}, bf16[4,128,768]{2,1,0:T(8,128)(2,1)S(1)}, u32[]{:S(2)}) copy-start(bf16[4,128,768]{2,1,0:T(8,128)(2,1)S(1)} %collective-permute-done.6.refs_1_.refs_2_) | copy-start | bytes 2359300
  63.9 18.4 %collective-permute-start.8 = (bf16[3,128,768]{2,1,0:T(8,128)(2,1)}, bf16[3,128,768]{2,1,0:T(8,128)(2,1)S(1)}, u32[]{:S(2)}, u32[]{:S(2)}) collective-permute-start(bf16[3,128,768]{2,1,0:T(8,128)(2,1)} %get-tuple-element.64), channel_id=1, source_target_pairs={{0,2},{1,3},{2,0},{3,1},{4,6},{5,7},{6,4},{7,5},{8,10},{9,11},{10,... | collective-permute-start | bytes 1769480 | tf_op jit(solution)/shard_map/ppermute | solution.py:879
  82.3 0.8 copy-start.1
where the time goes:
time: 87.6 us; the launch traced here: 87 us
  Pallas kernels  51.4 us (59%)
  blocking collectives  16.5 us (19%)
  starting transfers between devices  8.03 us (9%)
  waiting for transfers between devices  6.84 us (8%)
  local copies, waits for them, and re-layouts  3.32 us (4%)
  between operations  0.92 us (1%)
    pallas_call x5, Pallas kernels, call(): pl.pallas_call(kernel, out_shape=[jax.ShapeDtypeStruct(shape, dtype) for...  51.4 us
    all_to_all x1, blocking collectives, local(): lax.all_to_all(spread, axes, split_axis=0, concat_axis=0, tiled=True)  16.5 us
    ppermute x1, waiting for transfers between devices, local(): tf = lax.ppermute(picked.tf, 'mp', chip)  3.5 us
    unnamed x18, local copies, waits for them, and re-layouts  3.32 us
    ppermute x1, starting transfers between devices, local(): wf = lax.ppermute(picked.xf, 'mp', chip)  2.58 us
    ppermute x1, waiting for transfers between devices, local(): others = lax.ppermute(main.small, 'mp', core)  2 us
    ppermute x1, starting transfers between devices, local(): tf = lax.ppermute(picked.tf, 'mp', chip)  1.95 us
    ppermute x1, starting transfers between devices, local(): back = lax.ppermute(away, 'mp', chip)  1.83 us
  transfers between devices with their start and end apart: 9, of which 3 were waited for; matrix products, arithmetic and copies ran while one was open for 0% of the time, Pallas kernels for 9%

commit v1 on v0

--- a/solution.py
+++ b/solution.py
@@ -178,6 +178,8 @@
     w = worked(my_mp())
     blk = r.x.shape[1]
     mover = Mover(r.sems)
+    seq = 4 * blk
+    edges = start_edges(r, mover, seq)
     copies = [
         mover.start(src, dst)
         for src, dst in (
@@ -197,6 +199,9 @@
         r.left[n] = one.left
         r.fac[n] = one.fac
         r.right[n] = one.right
+    for copy in edges:
+        copy.wait()
+    fill_bias(r, bucket_hots(r, seq), blk)
     gain = gain_row(r.gain1)
     for copy in copies[:4]:
         copy.wait()
@@ -256,23 +261,24 @@
     blk = q.shape[0] // count
     low_half = iota((blk, LANES), 1) < HALF
     scores = dot(by_head(q[...]), k[...], 1, 1)
-    for u in range(2 * count):
-        h, b = divmod(u, count)
-        rows = slice(u * blk, (u + 1) * blk)
+    step = blk // 2
+    for u in range(4 * count):
+        h, b = divmod(u // 2, count)
+        rows = slice(u * step, (u + 1) * step)
+        q_rows = slice((u % 2) * step, (u % 2 + 1) * step)
         parts = []
         for n in range(4):
             place = pl.ds(pl.multiple_of((slots[n] - q_poss[b] + 3) * blk, blk), blk)
             parts.append(
-                scores[rows, n * blk : (n + 1) * blk] + (bias[2 * hp + h, :, place] + mask[n])
+                scores[rows, n * blk : (n + 1) * blk] + (bias[2 * hp + h, q_rows, place] + mask[n])
             )
         top = jnp.max(
             jnp.maximum(jnp.maximum(parts[0], parts[1]), jnp.maximum(parts[2], parts[3])),
             axis=-1,
             keepdims=True,
         )
-        parts = [jnp.exp(part - top) for part in parts]
         for n in range(4):
-            p[rows, n * blk : (n + 1) * blk] = parts[n].astype(BF16)
+            p[rows, n * blk : (n + 1) * blk] = jnp.exp(parts[n] - top).astype(BF16)
     values = v[...]
     out = dot(p[...], jnp.concatenate([values, jnp.ones_like(values)], axis=1))
     inv_all = 1.0 / out[:, LANES:]
@@ -332,6 +338,7 @@
         )
     )
     weights_kv = go(((r.wk_hbm, r.wk), (r.wv_hbm, r.wv), (r.wq_hbm, r.wq)))
+    toeplitz = mover.start(r.bias_hbm, r.bias)
     shared = go(
         (
             (r.q0.at[at(0)], r.q_s.at[at(0)]),
@@ -352,7 +359,6 @@
     for copy in edges:
         copy.wait()
     buckets = bucket_hots(r, seq)
-    fill_bias(r, buckets, blk)
     for n in range(4):
         far_rows[n].wait()
         r.far[at(n)] = normed(r.rows[at(2 * n + 1)], gain1)
@@ -382,6 +388,7 @@
     r.q_s[at(1)] = dot(r.far[at(0)], r.wq[...]).astype(BF16)
     for copy in shared:
         copy.wait()
+    toeplitz.wait()
     masks = [key_masks(slots, r.lengths[n], blk) for n in (w, 1)]
     groups = (
         (slice(0, 2 * blk), (mp, mp ^ 2), slice(0, seq), r.pw_s),
@@ -510,10 +517,16 @@
         for h in range(2):
             near = scores[0][2 * h * blk : (2 * h + 1) * blk] + scores[1][h * blk : (h + 1) * blk]
             far = scores[0][(2 * h + 1) * blk : (2 * h + 2) * blk]
-            for piece, q_pos in ((near, mp), (far, mp ^ 2)):
+            for piece, q_pos, away in ((near, mp, 1), (far, mp ^ 2, 0)):
                 for n in range(4):
                     place = pl.ds(pl.multiple_of((slots[n] - q_pos + 3) * blk, blk), blk)
-                    acc[2 * hp + h, :, place] += piece[:, n * blk : (n + 1) * blk]
+                    add = piece[:, n * blk : (n + 1) * blk]
+                    if n == away:
+                        acc[2 * hp + h, 0:8, place] += jnp.sum(
+                            add.reshape(blk // 8, 8, blk), axis=0
+                        )
+                    else:
+                        acc[2 * hp + h, :, place] += add
 
     sub = iota((8, seq), 0)
 
@@ -548,12 +561,14 @@
     for first, dq_rows in ((0, slice(0, 2 * blk)), (4, at(2))):
         cols = slice(first * blk, first * blk + seq)
         pieces = []
+        dk = r.dkt[:, cols].T
+        dv = r.dvt[:, cols].T
         for n in range(width // side):
             outs = slice(n * side, (n + 1) * side)
-            piece = dot(r.dkt[:, cols], r.wk[outs, :], 0, 1)
+            piece = dot(dk, r.wk[outs, :], 1, 1)
             if len(sums) < heads:
                 sums.append(along_diagonals(len(sums)))
-            piece = piece + dot(r.dvt[:, cols], r.wv[outs, :], 0, 1)
+            piece = piece + dot(dv, r.wv[outs, :], 1, 1)
             if len(sums) < heads:
                 sums.append(along_diagonals(len(sums)))
             pieces.append(piece)
@@ -620,7 +635,6 @@
             (r.recv.at[1], r.recv_s.at[0]),
             (r.base.at[3], r.base_s.at[1]),
             (r.recv.at[3], r.recv_s.at[1]),
-            (r.blk_f, r.away.at[2]),
         )
     ]
     spread = r.small.shape[0] // 2
@@ -639,7 +653,6 @@
         copies[2 * n].wait()
         copies[2 * n + 1].wait()
         r.away[n] = (r.base_s[n] + r.recv_s[n].astype(F32)).astype(BF16)
-    copies[4].wait()
 
 
 def finish_body(token_total, seq_total, r):
@@ -656,7 +669,7 @@
             (r.recv.at[0], r.recv_s.at[0]),
             (r.base.at[2], r.base_s.at[1]),
             (r.recv.at[2], r.recv_s.at[1]),
-            (r.back.at[2], r.block.at[2 - w]),
+            (r.blk_f, r.block.at[2 - w]),
             (r.blk_own.at[0], r.block.at[w]),
             (r.blk_own.at[1], r.block.at[1]),
         )
@@ -763,6 +776,8 @@
             ("dr", down_right, VMEM),
             ("ul", up_left, VMEM),
             ("ur", up_right, VMEM),
+            ("table", table, VMEM),
+            ("bucket", relative_bucket, HBM),
             ("wq_hbm", query_matrix, HBM),
             ("wk_hbm", key_matrix, HBM),
             ("wv_hbm", value_matrix, HBM),
@@ -775,9 +790,10 @@
             ("left", (2, kron * kron, width), F32, VMEM),
             ("fac", (2, kron * kron, LANES), F32, VMEM),
             ("right", (2, kron * kron, LANES), F32, VMEM),
+            ("bias", (heads, blk, 7 * blk), F32, VMEM),
         ],
-        {"rows": rows(4), "xn": rows(4), "wq": square, "wk": square, "wv": square},
-        7,
+        {"edge": ((2, 8, seq), jnp.int32), "rows": rows(4), "xn": rows(4), "wq": square, "wk": square, "wv": square},
+        9,
         4.0,
     )
 
@@ -806,6 +822,7 @@
             ("gain2", ffn_gain, VMEM),
             ("table", table, VMEM),
             ("bucket", relative_bucket, HBM),
+            ("bias_hbm", prep.bias, HBM),
             ("low", prep.low, VMEM),
             ("left", prep.left, VMEM),
             ("fac", prep.fac, VMEM),
@@ -861,7 +878,7 @@
             "base_s": rows(4, F32),
             "send_s": rows(4),
         },
-        44,
+        45,
         28.0,
     )
     recv = lax.ppermute(main.send, "mp", core)
@@ -870,13 +887,14 @@
     middle = call(
         "middle",
         middle_body,
-        [("base", main.base, HBM), ("recv", recv, HBM), ("blk_f", main.blk_f, HBM), ("small", main.small, VMEM), ("others", others, VMEM)],
-        [("away", (3, blk, width), BF16, VMEM), ("spread", (devices, 16, LANES), BF16, VMEM)],
+        [("base", main.base, HBM), ("recv", recv, HBM), ("small", main.small, VMEM), ("others", others, VMEM)],
+        [("away", (2, blk, width), BF16, VMEM), ("spread", (devices, 16, LANES), BF16, VMEM)],
         {"base_s": pair(F32), "recv_s": pair(BF16)},
-        5,
-    )
-    spread, away = lax.optimization_barrier((middle.spread, middle.away))
-    back = lax.ppermute(away, "mp", chip)
+        4,
+    )
+    back = lax.ppermute(middle.away, "mp", chip)
+    blk_f = lax.ppermute(main.blk_f, "mp", chip)
+    spread, blk_f = lax.optimization_barrier((middle.spread, blk_f))
     gathered = lax.all_to_all(spread, axes, split_axis=0, concat_axis=0, tiled=True)
 
     done = call(
@@ -888,6 +906,7 @@
             ("recv", recv, HBM),
             ("back", back, HBM),
             ("blk_own", main.blk_own, HBM),
+            ("blk_f", blk_f, HBM),
             ("fac", factors, VMEM),
             ("dl", down_left, VMEM),
             ("dr", down_right, VMEM),

time: 87.6 us -> 84.3 us (0.962)
  waiting for transfers between devices: 6.84 us -> 2.9 us
  blocking collectives: 16.5 us -> 13.9 us
  Pallas kernels: 51.4 us -> 53.8 us
    all_to_all x1, blocking collectives: 16.5 us -> 13.9 us  [local(): lax.all_to_all(spread, axes, split_axis=0, concat_axis=0, tiled=True)]
    pallas_call x5, Pallas kernels: 51.4 us -> 53.8 us  [call(): pl.pallas_call(kernel, out_shape=[jax.ShapeDtypeStruct(shape, dtype) for...]
    ppermute x1, waiting for transfers between devices: 3.5 us -> 1.66 us  [local(): tf = lax.ppermute(picked.tf, 'mp', chip)]
    ppermute x1, waiting for transfers between devices: 1.33 us -> 0.01 us  [local(): cx = lax.ppermute(picked.xc, 'mp', chip)]
    ppermute x1 -> x2, starting transfers between devices: 1.83 us -> 2.94 us  [the longest x1 1.83 us: local(): blk_f = lax.ppermute(main.blk_f, 'mp', chip)]
    unnamed x18 -> x20, local copies, waits for them, and re-layouts: 3.32 us -> 3.23 us
  transfers between devices with their start and end apart: 9 -> 10, of which waited for: 3 -> 2; matrix products, arithmetic and copies ran while one was open for 0% -> 0% of each run, Pallas kernels for 9% -> 17%
where the time goes in v1:
time: 84.3 us; the launch traced here: 83.7 us
  Pallas kernels  53.8 us (64%)
  blocking collectives  13.9 us (16%)
  starting transfers between devices  8.87 us (11%)
  local copies, waits for them, and re-layouts  3.23 us (4%)
  waiting for transfers between devices  2.9 us (3%)
  between operations  0.95 us (1%)
    pallas_call x5, Pallas kernels, call(): pl.pallas_call(kernel, out_shape=[jax.ShapeDtypeStruct(shape, dtype) for...  53.8 us
    all_to_all x1, blocking collectives, local(): lax.all_to_all(spread, axes, split_axis=0, concat_axis=0, tiled=True)  13.9 us
    unnamed x20, local copies, waits for them, and re-layouts  3.23 us
    ppermute x1, starting transfers between devices, local(): wf = lax.ppermute(picked.xf, 'mp', chip)  2.58 us
    ppermute x1, starting transfers between devices, local(): tf = lax.ppermute(picked.tf, 'mp', chip)  1.95 us
    ppermute x1, starting transfers between devices, local(): blk_f = lax.ppermute(main.blk_f, 'mp', chip)  1.83 us
  transfers between devices with their start and end apart: 10, of which 2 were waited for; matrix products, arithmetic and copies ran while one was open for 0% of the time, Pallas kernels for 17%

profile of v1, /device:TPU:0, one launch (start us, length us, event | category | flops | bytes accessed | tf_op | source)
XLA Modules:
  0.0 83.7 jit_solution(8251999887548283946)
XLA Ops:
  0.6 0.5 collective-permute-start.2
  1.2 2.0 %pick.1 = (bf16[128,768]{1,0:T(8,128)(2,1)}, bf16[128,768]{1,0:T(8,128)(2,1)}, bf16[128,768]{1,0:T(8,128)(2,1)}) custom-call(bf16[3,128,768]{2,1,0:T(8,128)(2,1)} %refs_1_.3, bf16[3,128,768]{2,1,0:T(8,128)(2,1)} %refs_2_.3), custom_call_target="tpu_custom_call" | custom-call | tf_op jit(solution)/shard_map/pick/pallas_call | solution.py:69
  3.2 2.6 %collective-permute-start = (bf16[128,768]{1,0:T(8,128)(2,1)}, bf16[128,768]{1,0:T(8,128)(2,1)S(1)}, u32[]{:S(2)}, u32[]{:S(2)}) collective-permute-start(bf16[128,768]{1,0:T(8,128)(2,1)} %get-tuple-element.45), channel_id=1, source_target_pairs={{0,2},{1,3},{2,0},{3,1},{4,6},{5,7},{6,4},{7,5},{8,10},{9,11},{10,... | collective-permute-start | bytes 589832 | tf_op jit(solution)/shard_map/ppermute | solution.py:763
  5.8 0.1 collective-permute-start.1
  5.8 1.9 %collective-permute-start.3 = (bf16[128,768]{1,0:T(8,128)(2,1)}, bf16[128,768]{1,0:T(8,128)(2,1)S(1)}, u32[]{:S(2)}, u32[]{:S(2)}) collective-permute-start(bf16[128,768]{1,0:T(8,128)(2,1)} %get-tuple-element.50), channel_id=1, source_target_pairs={{0,2},{1,3},{2,0},{3,1},{4,6},{5,7},{6,4},{7,5},{8,10},{9,11},{10,... | collective-permute-start | bytes 589832 | tf_op jit(solution)/shard_map/ppermute | solution.py:765
  7.8 0.0 collective-permute-done.2.refs_1_.refs_6_
  7.8 0.8 copy-done.4
  8.6 9.1 %prep.1 = (bf16[256,768]{1,0:T(8,128)(2,1)}, bf16[512,768]{1,0:T(8,128)(2,1)}, bf16[512,768]{1,0:T(8,128)(2,1)}, bf16[2,768,128]{2,1,0:T(8,128)(2,1)}, f32[2,16,...) custom-call(bf16[3,128,768]{2,1,0:T(8,128)(2,1)} %refs_1_.3, ...), custom_call_target="tpu_custom_call" | custom-call | flops 4000000000 | tf_op jit(solution)/shard_map/prep/pallas_call | solution.py:69
  17.7 0.0 collective-permute-done.refs_3_
  17.7 0.0 collective-permute-done.1.refs_4_
  17.7 0.1 collective-permute-start.4
  17.8 0.5 collective-permute-start.5
  18.3 1.7 %collective-permute-done.3.refs_5_ = bf16[128,768]{1,0:T(8,128)(2,1)S(1)} collective-permute-done((bf16[128,768]{1,0:T(8,128)(2,1)}, bf16[128,768]{1,0:T(8,128)(2,1)S(1)}, u32[]{:S(2)}, u32[]{:S(2)}) %collective-permute-start.3) | collective-permute-done | bytes 196640 | tf_op jit(solution)/shard_map/ppermute | solution.py:765
  20.0 0.0 collective-permute-done.4.refs_7_
  20.0 0.0 collective-permute-done.5.refs_8_
  20.0 0.7 copy-done.7
  20.7 0.1 copy-done.8
  20.7 0.1 copy-done.9
  20.8 36.1 %main.1 = (bf16[2,128,768]{2,1,0:T(8,128)(2,1)}, bf16[128,768]{1,0:T(8,128)(2,1)}, f32[4,128,768]{2,1,0:T(8,128)}, bf16[4,128,768]{2,1,0:T(8,128)(2,1)}, bf16[32,128]{1,0:T(8,128)(2,1)}) custom-call(s32[3]{0:T(128)} %refs_0_.5, bf16[3,128,768]{2,1,0:T(8,128)(2,1)} %refs_1_.3, bf16[3,128,768]{2,1,0:T(8,128)(2,1)} %refs_2_.3, bf16[128,768]{1,0:T(8,128)(2,1)} %copy-done.5, ...), custom_call_target="tpu_custom_call" | custom-call | flops 28000000000 | tf_op jit(solution)/shard_map/main/pallas_call | solution.py:69
  56.9 0.1 collective-permute-start.6
  57.0 1.8 %collective-permute-start.8 = (bf16[128,768]{1,0:T(8,128)(2,1)}, bf16[128,768]{1,0:T(8,128)(2,1)S(1)}, u32[]{:S(2)}, u32[]{:S(2)}) collective-permute-start(bf16[128,768]{1,0:T(8,128)(2,1)} %get-tuple-element.63), channel_id=1, source_target_pairs={{0,2},{1,3},{2,0},{3,1},{4,6},{5,7},{6,4},{7,5},{8,10},{9,11},{10,... | collective-permute-start | bytes 589832 | tf_op jit(solution)/shard_map/ppermute | solution.py:896
  58.8 0.2 collective-permute-start.7
  59.0 1.2 %collective-permute-done.7.refs_3_ = bf16[32,128]{1,0:T(8,128)(2,1)S(1)} collective-permute-done((bf16[32,128]{1,0:T(8,128)(2,1)}, bf16[32,128]{1,0:T(8,128)(2,1)S(1)}, u32[]{:S(2)}, u32[]{:S(2)}) %collective-permute-start.7) | collective-permute-done | bytes 8224 | tf_op jit(solution)/shard_map/ppermute | solution.py:885
  60.2 0.0 collective-permute-done.6.refs_1_.refs_2_
  60.2 0.6 copy-done.3
  60.8 0.3 copy-done
  61.1 2.8 %middle.1 = (bf16[2,128,768]{2,1,0:T(8,128)(2,1)}, bf16[32,16,128]{2,1,0:T(8,128)(2,1)}) custom-call(f32[4,128,768]{2,1,0:T(8,128)} %get-tuple-element.59.refs_0_.refs_1_, bf16[4,128,768]{2,1,0:T(8,128)(2,1)} %copy-done, bf16[32,128]{1,0:T(8,128)(2,1)} %get-tuple-element.61.refs_2_, bf16[32,128]{1,0:T(8,128)(2,1)} %copy-done.3), custom_call_target="tpu_custom_call" | custom-call | tf_op jit(solution)/shard_map/middle/pallas_call | solution.py:69
  63.9 1.1 %collective-permute-start.9 = (bf16[2,128,768]{2,1,0:T(8,128)(2,1)}, bf16[2,128,768]{2,1,0:T(8,128)(2,1)S(1)}, u32[]{:S(2)}, u32[]{:S(2)}) collective-permute-start(bf16[2,128,768]{2,1,0:T(8,128)(2,1)} %get-tuple-element.65), channel_id=1, source_target_pairs={{0,2},{1,3},{2,0},{3,1},{4,6},{5,7},{6,4},{7,5},{8,10},{9,11},{10,... | collective-permute-start | bytes 1179656 | tf_op jit(solution)/shard_map/ppermute | solution.py:895
  65.0 0.0 collective-permute-done.8.refs_5_
  65.0 13.9 %all_to_all.5.refs_0_ = bf16[32,16,128]{2,1,0:T(8,128)(2,1)} all-to-all(bf16[32,16,128]{2,1,0:T(8,128)(2,1)} %get-tuple-element.64), channel_id=1, replica_groups=mesh['dp'=8,'mp'=4] {'dp','mp'}, dimensions={0} | all-to-all | bytes 262144 | tf_op jit(solution)/shard_map/all_to_all | solution.py:898
  79.0 0.7 copy-done.1
  79.7 3.8 %finish.1 = (f32[1,1]{1,0:T(1,128)}, bf16[3,128,768]{2,1,0:T(8,128)(2,1)}, f32[3,128,768]{2,1,0:T(8,128)}, f32[6,128]{1,0:T(8,128)}, f32[6,128]{1,0:T(8,128)}, /...) custom-call(bf16[32,16,128]{2,1,0:T(8,128)(2,1)} %all_to_all.5.refs_, ...), custom_call_target="tpu_custom_call" | custom-call | tf_op jit(solution)/shard_map/finish/pallas_call | solution.py:69
  (14 shorter events, 0.0 us)
Async XLA Ops:
  0.6 7.2 %collective-permute-start.2 = (bf16[3,128,768]{2,1,0:T(8,128)(2,1)}, bf16[3,128,768]{2,1,0:T(8,128)(2,1)S(1)}, u32[]{:S(2)}, u32[]{:S(2)}) collective-permute-start(bf16[3,128,768]{2,1,0:T(8,128)(2,1)} %refs_1_.3), channel_id=1, source_target_pairs={{0,1},{1,0},{2,3},{3,2},{4,5},{5,4},{6,7},{7,6},{8,9},{9,8},{10,11... | collective-permute-start | bytes 1769480 | tf_op jit(solution)/shard_map/ppermute | solution.py:766
  3.2 14.5 %collective-permute-start = (bf16[128,768]{1,0:T(8,128)(2,1)}, bf16[128,768]{1,0:T(8,128)(2,1)S(1)}, u32[]{:S(2)}, u32[]{:S(2)}) collective-permute-start(bf16[128,768]{1,0:T(8,128)(2,1)} %get-tuple-element.45), channel_id=1, source_target_pairs={{0,2},{1,3},{2,0},{3,1},{4,6},{5,7},{6,4},{7,5},{8,10},{9,11},{10,... | collective-permute-start | bytes 589832 | tf_op jit(solution)/shard_map/ppermute | solution.py:763
  5.8 11.9 %collective-permute-start.1 = (bf16[128,768]{1,0:T(8,128)(2,1)}, bf16[128,768]{1,0:T(8,128)(2,1)S(1)}, u32[]{:S(2)}, u32[]{:S(2)}) collective-permute-start(bf16[128,768]{1,0:T(8,128)(2,1)} %get-tuple-element.46), channel_id=1, source_target_pairs={{0,2},{1,3},{2,0},{3,1},{4,6},{5,7},{6,4},{7,5},{8,10},{9,11},{10,... | collective-permute-start | bytes 589832 | tf_op jit(solution)/shard_map/ppermute | solution.py:764
  5.8 14.1 %collective-permute-start.3 = (bf16[128,768]{1,0:T(8,128)(2,1)}, bf16[128,768]{1,0:T(8,128)(2,1)S(1)}, u32[]{:S(2)}, u32[]{:S(2)}) collective-permute-start(bf16[128,768]{1,0:T(8,128)(2,1)} %get-tuple-element.50), channel_id=1, source_target_pairs={{0,2},{1,3},{2,0},{3,1},{4,6},{5,7},{6,4},{7,5},{8,10},{9,11},{10,... | collective-permute-start | bytes 589832 | tf_op jit(solution)/shard_map/ppermute | solution.py:765
  7.8 0.8 copy-start.4
  17.7 2.3 %copy-start.5 = (bf16[128,768]{1,0:T(8,128)(2,1)}, bf16[128,768]{1,0:T(8,128)(2,1)S(1)}, u32[]{:S(2)}) copy-start(bf16[128,768]{1,0:T(8,128)(2,1)S(1)} %collective-permute-done.refs_3_) | copy-start | bytes 589828
  17.7 2.3 %copy-start.6 = (bf16[128,768]{1,0:T(8,128)(2,1)}, bf16[128,768]{1,0:T(8,128)(2,1)S(1)}, u32[]{:S(2)}) copy-start(bf16[128,768]{1,0:T(8,128)(2,1)S(1)} %collective-permute-done.1.refs_4_) | copy-start | bytes 589828
  17.7 2.2 %collective-permute-start.4 = (bf16[128,768]{1,0:T(8,128)(2,1)S(1)}, bf16[128,768]{1,0:T(8,128)(2,1)S(1)}, u32[]{:S(2)}, u32[]{:S(2)}) collective-permute-start(bf16[128,768]{1,0:T(8,128)(2,1)S(1)} %collective-permute-done.refs_3_), channel_id=1, source_target_pairs={{0,1},{1,0},{2,3},{3,2},{4,5},{5,4},{6,7},{7,6},{8,9},{9,8},{10,11... | collective-permute-start | bytes 589832 | tf_op jit(solution)/shard_map/ppermute | solution.py:801
  17.8 2.2 %collective-permute-start.5 = (bf16[128,768]{1,0:T(8,128)(2,1)S(1)}, bf16[128,768]{1,0:T(8,128)(2,1)S(1)}, u32[]{:S(2)}, u32[]{:S(2)}) collective-permute-start(bf16[128,768]{1,0:T(8,128)(2,1)S(1)} %collective-permute-done.1.refs_4_), channel_id=1, source_target_pairs={{0,1},{1,0},{2,3},{3,2},{4,5},{5,4},{6,7},{7,6},{8,9},{9,8},{10,11... | collective-permute-start | bytes 589832 | tf_op jit(solution)/shard_map/ppermute | solution.py:802
  20.0 0.7 copy-start.7
  20.0 0.7 copy-start.8
  20.0 0.8 copy-start.9
  56.9 3.3 %collective-permute-start.6 = (bf16[4,128,768]{2,1,0:T(8,128)(2,1)}, bf16[4,128,768]{2,1,0:T(8,128)(2,1)S(1)}, u32[]{:S(2)}, u32[]{:S(2)}) collective-permute-start(bf16[4,128,768]{2,1,0:T(8,128)(2,1)} %get-tuple-element.60), channel_id=1, source_target_pairs={{0,1},{1,0},{2,3},{3,2},{4,5},{5,4},{6,7},{7,6},{8,9},{9,8},{10,11... | collective-permute-start | bytes 2359304 | tf_op jit(solution)/shard_map/ppermute | solution.py:884
  57.0 8.0 %collective-permute-start.8 = (bf16[128,768]{1,0:T(8,128)(2,1)}, bf16[128,768]{1,0:T(8,128)(2,1)S(1)}, u32[]{:S(2)}, u32[]{:S(2)}) collective-permute-start(bf16[128,768]{1,0:T(8,128)(2,1)} %get-tuple-element.63), channel_id=1, source_target_pairs={{0,2},{1,3},{2,0},{3,1},{4,6},{5,7},{6,4},{7,5},{8,10},{9,11},{10,... | collective-permute-start | bytes 589832 | tf_op jit(solution)/shard_map/ppermute | solution.py:896
  58.8 1.4 %collective-permute-start.7 = (bf16[32,128]{1,0:T(8,128)(2,1)}, bf16[32,128]{1,0:T(8,128)(2,1)S(1)}, u32[]{:S(2)}, u32[]{:S(2)}) collective-permute-start(bf16[32,128]{1,0:T(8,128)(2,1)} %get-tuple-element.61.refs_2_), channel_id=1, source_target_pairs={{0,1},{1,0},{2,3},{3,2},{4,5},{5,4},{6,7},{7,6},{8,9},{9,8},{10,11... | collective-permute-start | bytes 24584 | tf_op jit(solution)/shard_map/ppermute | solution.py:885
  60.2 0.6 copy-start.3
  60.2 0.9 %copy-start = (bf16[4,128,768]{2,1,0:T(8,128)(2,1)}, bf16[4,128,768]{2,1,0:T(8,128)(2,1)S(1)}, u32[]{:S(2)}) copy-start(bf16[4,128,768]{2,1,0:T(8,128)(2,1)S(1)} %collective-permute-done.6.refs_1_.refs_2_) | copy-start | bytes 2359300
  63.9 15.1 %collective-permute-start.9 = (bf16[2,128,768]{2,1,0:T(8,128)(2,1)}, bf16[2,128,768]{2,1,0:T(8,128)(2,1)S(1)}, u32[]{:S(2)}, u32[]{:S(2)}) collective-permute-start(bf16[2,128,768]{2,1,0:T(8,128)(2,1)} %get-tuple-element.65), channel_id=1, source_target_pairs={{0,2},{1,3},{2,0},{3,1},{4,6},{5,7},{6,4},{7,5},{8,10},{9,11},{10,... | collective-permute-start | bytes 1179656 | tf_op jit(solution)/shard_map/ppermute | solution.py:895
  65.0 14.0 %copy-start.2 = (bf16[128,768]{1,0:T(8,128)(2,1)}, bf16[128,768]{1,0:T(8,128)(2,1)S(1)}, u32[]{:S(2)}) copy-start(bf16[128,768]{1,0:T(8,128)(2,1)S(1)} %collective-permute-done.8.refs_5_) | copy-start | bytes 589828
  79.0 0.7 copy-start.1

commit v2 on v1

--- a/solution.py
+++ b/solution.py
@@ -16,7 +16,7 @@
 GELU_B = 0.044715
 LANES = 128
 HALF = LANES // 2
-VMEM_BYTES = 62 * 2**20
+VMEM_BYTES = 64 * 2**20 - 2**17
 HBM = pltpu.HBM
 VMEM = pltpu.VMEM
 SMEM = pltpu.SMEM

time: 84.3 us -> 82.8 us (0.982)
  local copies, waits for them, and re-layouts: 3.23 us -> 0.59 us
  waiting for transfers between devices: 2.9 us -> 3.84 us
    unnamed x20 -> x2, local copies, waits for them, and re-layouts: 3.23 us -> 0.59 us
    ppermute x1, waiting for transfers between devices: 1.66 us -> 2.6 us  [local(): tf = lax.ppermute(picked.tf, 'mp', chip)]
where the time goes in v2:
time: 82.8 us; the launch traced here: 82.3 us
  Pallas kernels  53.8 us (65%)
  blocking collectives  14.3 us (17%)
  starting transfers between devices  8.87 us (11%)
  waiting for transfers between devices  3.84 us (5%)
  between operations  0.9 us (1%)
    pallas_call x5, Pallas kernels, call(): pl.pallas_call(kernel, out_shape=[jax.ShapeDtypeStruct(shape, dtype) for...  53.8 us
    all_to_all x1, blocking collectives, local(): lax.all_to_all(spread, axes, split_axis=0, concat_axis=0, tiled=True)  14.3 us
    ppermute x1, waiting for transfers between devices, local(): tf = lax.ppermute(picked.tf, 'mp', chip)  2.6 us
    ppermute x1, starting transfers between devices, local(): wf = lax.ppermute(picked.xf, 'mp', chip)  2.58 us
    ppermute x1, starting transfers between devices, local(): tf = lax.ppermute(picked.tf, 'mp', chip)  1.95 us
    ppermute x1, starting transfers between devices, local(): blk_f = lax.ppermute(main.blk_f, 'mp', chip)  1.83 us
  transfers between devices with their start and end apart: 10, of which 2 were waited for; matrix products, arithmetic and copies ran while one was open for 0% of the time, Pallas kernels for 17%

profile of v2, /device:TPU:0, one launch (start us, length us, event | category | flops | bytes accessed | tf_op | source)
XLA Modules:
  0.0 82.3 jit_solution(16387895464415788456)
XLA Ops:
  0.6 0.5 collective-permute-start.2
  1.2 2.0 %pick.1 = (bf16[128,768]{1,0:T(8,128)(2,1)}, bf16[128,768]{1,0:T(8,128)(2,1)}, bf16[128,768]{1,0:T(8,128)(2,1)}) custom-call(bf16[3,128,768]{2,1,0:T(8,128)(2,1)} %refs_1_.3, bf16[3,128,768]{2,1,0:T(8,128)(2,1)} %refs_2_.3), custom_call_target="tpu_custom_call" | custom-call | tf_op jit(solution)/shard_map/pick/pallas_call | solution.py:69
  3.1 2.6 %collective-permute-start = (bf16[128,768]{1,0:T(8,128)(2,1)}, bf16[128,768]{1,0:T(8,128)(2,1)}, u32[]{:S(2)}, u32[]{:S(2)}) collective-permute-start(bf16[128,768]{1,0:T(8,128)(2,1)} %get-tuple-element.45), channel_id=1, source_target_pairs={{0,2},{1,3},{2,0},{3,1},{4,6},{5,7},{6,4},{7,5},{8,10},{9,11},{10,... | collective-permute-start | bytes 589832 | tf_op jit(solution)/shard_map/ppermute | solution.py:763
  5.7 0.1 collective-permute-start.1
  5.8 1.9 %collective-permute-start.3 = (bf16[128,768]{1,0:T(8,128)(2,1)}, bf16[128,768]{1,0:T(8,128)(2,1)}, u32[]{:S(2)}, u32[]{:S(2)}) collective-permute-start(bf16[128,768]{1,0:T(8,128)(2,1)} %get-tuple-element.50), channel_id=1, source_target_pairs={{0,2},{1,3},{2,0},{3,1},{4,6},{5,7},{6,4},{7,5},{8,10},{9,11},{10,... | collective-permute-start | bytes 589832 | tf_op jit(solution)/shard_map/ppermute | solution.py:765
  7.7 0.0 collective-permute-done.2.refs_1_.refs_6_
  7.7 9.1 %prep.1 = (bf16[256,768]{1,0:T(8,128)(2,1)}, bf16[512,768]{1,0:T(8,128)(2,1)}, bf16[512,768]{1,0:T(8,128)(2,1)}, bf16[2,768,128]{2,1,0:T(8,128)(2,1)}, f32[2,16,...) custom-call(bf16[3,128,768]{2,1,0:T(8,128)(2,1)} %refs_1_.3, ...), custom_call_target="tpu_custom_call" | custom-call | flops 4000000000 | tf_op jit(solution)/shard_map/prep/pallas_call | solution.py:69
  16.8 0.0 collective-permute-done.refs_3_
  16.8 0.0 collective-permute-done.1.refs_4_
  16.8 0.1 collective-permute-start.4
  16.9 0.5 collective-permute-start.5
  17.4 2.6 %collective-permute-done.3.refs_5_ = bf16[128,768]{1,0:T(8,128)(2,1)} collective-permute-done((bf16[128,768]{1,0:T(8,128)(2,1)}, bf16[128,768]{1,0:T(8,128)(2,1)}, u32[]{:S(2)}, u32[]{:S(2)}) %collective-permute-start.3) | collective-permute-done | bytes 196640 | tf_op jit(solution)/shard_map/ppermute | solution.py:765
  20.0 0.0 collective-permute-done.4.refs_7_
  20.0 0.0 collective-permute-done.5.refs_8_
  20.0 36.2 %main.1 = (bf16[2,128,768]{2,1,0:T(8,128)(2,1)}, bf16[128,768]{1,0:T(8,128)(2,1)}, f32[4,128,768]{2,1,0:T(8,128)}, bf16[4,128,768]{2,1,0:T(8,128)(2,1)}, bf16[32,128]{1,0:T(8,128)(2,1)}) custom-call(s32[3]{0:T(128)} %refs_0_.5, bf16[3,128,768]{2,1,0:T(8,128)(2,1)} %refs_1_.3, bf16[3,128,768]{2,1,0:T(8,128)(2,1)} %refs_2_.3, ...), custom_call_target="tpu_custom_call" | custom-call | flops 28000000000 | tf_op jit(solution)/shard_map/main/pallas_call | solution.py:69
  56.2 0.1 collective-permute-start.6
  56.3 1.8 %collective-permute-start.8 = (bf16[128,768]{1,0:T(8,128)(2,1)}, bf16[128,768]{1,0:T(8,128)(2,1)}, u32[]{:S(2)}, u32[]{:S(2)}) collective-permute-start(bf16[128,768]{1,0:T(8,128)(2,1)} %get-tuple-element.63), channel_id=1, source_target_pairs={{0,2},{1,3},{2,0},{3,1},{4,6},{5,7},{6,4},{7,5},{8,10},{9,11},{10,... | collective-permute-start | bytes 589832 | tf_op jit(solution)/shard_map/ppermute | solution.py:896
  58.1 0.2 collective-permute-start.7
  58.3 1.2 %collective-permute-done.7.refs_3_ = bf16[32,128]{1,0:T(8,128)(2,1)S(1)} collective-permute-done((bf16[32,128]{1,0:T(8,128)(2,1)}, bf16[32,128]{1,0:T(8,128)(2,1)S(1)}, u32[]{:S(2)}, u32[]{:S(2)}) %collective-permute-start.7) | collective-permute-done | bytes 8224 | tf_op jit(solution)/shard_map/ppermute | solution.py:885
  59.5 0.0 copy-start
  59.5 0.0 collective-permute-done.6.refs_1_.refs_2_
  59.5 0.6 copy-done
  60.1 2.8 %middle.1 = (bf16[2,128,768]{2,1,0:T(8,128)(2,1)}, bf16[32,16,128]{2,1,0:T(8,128)(2,1)}) custom-call(f32[4,128,768]{2,1,0:T(8,128)} %get-tuple-element.59.refs_0_.refs_1_, bf16[4,128,768]{2,1,0:T(8,128)(2,1)} %collective-permute-done.6.refs_1_.refs_2_, bf16[32,128]{1,0:T(8,128)(2,1)} %get-tuple-element.61.refs_2_, bf16[32,128]{1,0:T(8,128)(2,1)} %copy-done), custom_call_target="tpu_custom_call" | custom-call | tf_op jit(solution)/shard_map/middle/pallas_call | solution.py:69
  62.9 1.1 %collective-permute-start.9 = (bf16[2,128,768]{2,1,0:T(8,128)(2,1)}, bf16[2,128,768]{2,1,0:T(8,128)(2,1)}, u32[]{:S(2)}, u32[]{:S(2)}) collective-permute-start(bf16[2,128,768]{2,1,0:T(8,128)(2,1)} %get-tuple-element.65), channel_id=1, source_target_pairs={{0,2},{1,3},{2,0},{3,1},{4,6},{5,7},{6,4},{7,5},{8,10},{9,11},{10,... | collective-permute-start | bytes 1179656 | tf_op jit(solution)/shard_map/ppermute | solution.py:895
  64.0 0.0 collective-permute-done.8.refs_5_
  64.0 14.3 %all_to_all.5.refs_0_ = bf16[32,16,128]{2,1,0:T(8,128)(2,1)} all-to-all(bf16[32,16,128]{2,1,0:T(8,128)(2,1)} %get-tuple-element.64), channel_id=1, replica_groups=mesh['dp'=8,'mp'=4] {'dp','mp'}, dimensions={0} | all-to-all | bytes 262144 | tf_op jit(solution)/shard_map/all_to_all | solution.py:898
  78.3 0.0 collective-permute-done.9.refs_3_
  78.3 3.8 %finish.1 = (f32[1,1]{1,0:T(1,128)}, bf16[3,128,768]{2,1,0:T(8,128)(2,1)}, f32[3,128,768]{2,1,0:T(8,128)}, f32[6,128]{1,0:T(8,128)}, f32[6,128]{1,0:T(8,128)}, /...) custom-call(bf16[32,16,128]{2,1,0:T(8,128)(2,1)} %all_to_all.5.refs_, ...), custom_call_target="tpu_custom_call" | custom-call | tf_op jit(solution)/shard_map/finish/pallas_call | solution.py:69
Async XLA Ops:
  0.6 7.1 %collective-permute-start.2 = (bf16[3,128,768]{2,1,0:T(8,128)(2,1)}, bf16[3,128,768]{2,1,0:T(8,128)(2,1)}, u32[]{:S(2)}, u32[]{:S(2)}) collective-permute-start(bf16[3,128,768]{2,1,0:T(8,128)(2,1)} %refs_1_.3), channel_id=1, source_target_pairs={{0,1},{1,0},{2,3},{3,2},{4,5},{5,4},{6,7},{7,6},{8,9},{9,8},{10,11... | collective-permute-start | bytes 1769480 | tf_op jit(solution)/shard_map/ppermute | solution.py:766
  3.1 13.7 %collective-permute-start = (bf16[128,768]{1,0:T(8,128)(2,1)}, bf16[128,768]{1,0:T(8,128)(2,1)}, u32[]{:S(2)}, u32[]{:S(2)}) collective-permute-start(bf16[128,768]{1,0:T(8,128)(2,1)} %get-tuple-element.45), channel_id=1, source_target_pairs={{0,2},{1,3},{2,0},{3,1},{4,6},{5,7},{6,4},{7,5},{8,10},{9,11},{10,... | collective-permute-start | bytes 589832 | tf_op jit(solution)/shard_map/ppermute | solution.py:763
  5.7 11.1 %collective-permute-start.1 = (bf16[128,768]{1,0:T(8,128)(2,1)}, bf16[128,768]{1,0:T(8,128)(2,1)}, u32[]{:S(2)}, u32[]{:S(2)}) collective-permute-start(bf16[128,768]{1,0:T(8,128)(2,1)} %get-tuple-element.46), channel_id=1, source_target_pairs={{0,2},{1,3},{2,0},{3,1},{4,6},{5,7},{6,4},{7,5},{8,10},{9,11},{10,... | collective-permute-start | bytes 589832 | tf_op jit(solution)/shard_map/ppermute | solution.py:764
  5.8 14.2 %collective-permute-start.3 = (bf16[128,768]{1,0:T(8,128)(2,1)}, bf16[128,768]{1,0:T(8,128)(2,1)}, u32[]{:S(2)}, u32[]{:S(2)}) collective-permute-start(bf16[128,768]{1,0:T(8,128)(2,1)} %get-tuple-element.50), channel_id=1, source_target_pairs={{0,2},{1,3},{2,0},{3,1},{4,6},{5,7},{6,4},{7,5},{8,10},{9,11},{10,... | collective-permute-start | bytes 589832 | tf_op jit(solution)/shard_map/ppermute | solution.py:765
  16.8 3.2 %collective-permute-start.4 = (bf16[128,768]{1,0:T(8,128)(2,1)}, bf16[128,768]{1,0:T(8,128)(2,1)}, u32[]{:S(2)}, u32[]{:S(2)}) collective-permute-start(bf16[128,768]{1,0:T(8,128)(2,1)} %collective-permute-done.refs_3_), channel_id=1, source_target_pairs={{0,1},{1,0},{2,3},{3,2},{4,5},{5,4},{6,7},{7,6},{8,9},{9,8},{10,11... | collective-permute-start | bytes 589832 | tf_op jit(solution)/shard_map/ppermute | solution.py:801
  16.9 3.1 %collective-permute-start.5 = (bf16[128,768]{1,0:T(8,128)(2,1)}, bf16[128,768]{1,0:T(8,128)(2,1)}, u32[]{:S(2)}, u32[]{:S(2)}) collective-permute-start(bf16[128,768]{1,0:T(8,128)(2,1)} %collective-permute-done.1.refs_4_), channel_id=1, source_target_pairs={{0,1},{1,0},{2,3},{3,2},{4,5},{5,4},{6,7},{7,6},{8,9},{9,8},{10,11... | collective-permute-start | bytes 589832 | tf_op jit(solution)/shard_map/ppermute | solution.py:802
  56.2 3.3 %collective-permute-start.6 = (bf16[4,128,768]{2,1,0:T(8,128)(2,1)}, bf16[4,128,768]{2,1,0:T(8,128)(2,1)}, u32[]{:S(2)}, u32[]{:S(2)}) collective-permute-start(bf16[4,128,768]{2,1,0:T(8,128)(2,1)} %get-tuple-element.60), channel_id=1, source_target_pairs={{0,1},{1,0},{2,3},{3,2},{4,5},{5,4},{6,7},{7,6},{8,9},{9,8},{10,11... | collective-permute-start | bytes 2359304 | tf_op jit(solution)/shard_map/ppermute | solution.py:884
  56.3 7.7 %collective-permute-start.8 = (bf16[128,768]{1,0:T(8,128)(2,1)}, bf16[128,768]{1,0:T(8,128)(2,1)}, u32[]{:S(2)}, u32[]{:S(2)}) collective-permute-start(bf16[128,768]{1,0:T(8,128)(2,1)} %get-tuple-element.63), channel_id=1, source_target_pairs={{0,2},{1,3},{2,0},{3,1},{4,6},{5,7},{6,4},{7,5},{8,10},{9,11},{10,... | collective-permute-start | bytes 589832 | tf_op jit(solution)/shard_map/ppermute | solution.py:896
  58.1 1.4 %collective-permute-start.7 = (bf16[32,128]{1,0:T(8,128)(2,1)}, bf16[32,128]{1,0:T(8,128)(2,1)S(1)}, u32[]{:S(2)}, u32[]{:S(2)}) collective-permute-start(bf16[32,128]{1,0:T(8,128)(2,1)} %get-tuple-element.61.refs_2_), channel_id=1, source_target_pairs={{0,1},{1,0},{2,3},{3,2},{4,5},{5,4},{6,7},{7,6},{8,9},{9,8},{10,11... | collective-permute-start | bytes 24584 | tf_op jit(solution)/shard_map/ppermute | solution.py:885
  59.5 0.6 copy-start
  62.9 15.4 %collective-permute-start.9 = (bf16[2,128,768]{2,1,0:T(8,128)(2,1)}, bf16[2,128,768]{2,1,0:T(8,128)(2,1)}, u32[]{:S(2)}, u32[]{:S(2)}) collective-permute-start(bf16[2,128,768]{2,1,0:T(8,128)(2,1)} %get-tuple-element.65), channel_id=1, source_target_pairs={{0,2},{1,3},{2,0},{3,1},{4,6},{5,7},{6,4},{7,5},{8,10},{9,11},{10,... | collective-permute-start | bytes 1179656 | tf_op jit(solution)/shard_map/ppermute | solution.py:895

commit v3 on v2

--- a/solution.py
+++ b/solution.py
@@ -16,7 +16,7 @@
 GELU_B = 0.044715
 LANES = 128
 HALF = LANES // 2
-VMEM_BYTES = 64 * 2**20 - 2**17
+VMEM_BYTES = 64 * 2**20 - 2**12
 HBM = pltpu.HBM
 VMEM = pltpu.VMEM
 SMEM = pltpu.SMEM

time: 82.8 us -> 82.9 us (level)
  transfers between devices with their start and end apart: 10 -> 10, of which waited for: 2 -> 3; matrix products, arithmetic and copies ran while one was open for 0% -> 0% of each run, Pallas kernels for 17% -> 17%
where the time goes in v3:
time: 82.9 us; the launch traced here: 82.3 us
  Pallas kernels  53.8 us (65%)
  blocking collectives  14.4 us (17%)
  starting transfers between devices  8.87 us (11%)
  waiting for transfers between devices  4.34 us (5%)
  between operations  0.89 us (1%)
    pallas_call x5, Pallas kernels, call(): pl.pallas_call(kernel, out_shape=[jax.ShapeDtypeStruct(shape, dtype) for...  53.8 us
    all_to_all x1, blocking collectives, local(): lax.all_to_all(spread, axes, split_axis=0, concat_axis=0, tiled=True)  14.4 us
    ppermute x1, waiting for transfers between devices, local(): tf = lax.ppermute(picked.tf, 'mp', chip)  2.6 us
    ppermute x1, starting transfers between devices, local(): wf = lax.ppermute(picked.xf, 'mp', chip)  2.58 us
    ppermute x1, starting transfers between devices, local(): tf = lax.ppermute(picked.tf, 'mp', chip)  1.95 us
    ppermute x1, starting transfers between devices, local(): blk_f = lax.ppermute(main.blk_f, 'mp', chip)  1.83 us
  transfers between devices with their start and end apart: 10, of which 3 were waited for; matrix products, arithmetic and copies ran while one was open for 0% of the time, Pallas kernels for 17%

profile of v3, /device:TPU:0, one launch (start us, length us, event | category | flops | bytes accessed | tf_op | source)
XLA Modules:
  0.0 82.3 jit_solution(13818792156285294009)
XLA Ops:
  0.6 0.5 collective-permute-start.2
  1.2 2.0 %pick.1 = (bf16[128,768]{1,0:T(8,128)(2,1)}, bf16[128,768]{1,0:T(8,128)(2,1)}, bf16[128,768]{1,0:T(8,128)(2,1)}) custom-call(bf16[3,128,768]{2,1,0:T(8,128)(2,1)} %refs_1_.3, bf16[3,128,768]{2,1,0:T(8,128)(2,1)} %refs_2_.3), custom_call_target="tpu_custom_call" | custom-call | tf_op jit(solution)/shard_map/pick/pallas_call | solution.py:69
  3.1 2.6 %collective-permute-start = (bf16[128,768]{1,0:T(8,128)(2,1)}, bf16[128,768]{1,0:T(8,128)(2,1)}, u32[]{:S(2)}, u32[]{:S(2)}) collective-permute-start(bf16[128,768]{1,0:T(8,128)(2,1)} %get-tuple-element.45), channel_id=1, source_target_pairs={{0,2},{1,3},{2,0},{3,1},{4,6},{5,7},{6,4},{7,5},{8,10},{9,11},{10,... | collective-permute-start | bytes 589832 | tf_op jit(solution)/shard_map/ppermute | solution.py:763
  5.7 0.1 collective-permute-start.1
  5.8 1.9 %collective-permute-start.3 = (bf16[128,768]{1,0:T(8,128)(2,1)}, bf16[128,768]{1,0:T(8,128)(2,1)}, u32[]{:S(2)}, u32[]{:S(2)}) collective-permute-start(bf16[128,768]{1,0:T(8,128)(2,1)} %get-tuple-element.50), channel_id=1, source_target_pairs={{0,2},{1,3},{2,0},{3,1},{4,6},{5,7},{6,4},{7,5},{8,10},{9,11},{10,... | collective-permute-start | bytes 589832 | tf_op jit(solution)/shard_map/ppermute | solution.py:765
  7.7 0.0 collective-permute-done.2.refs_1_.refs_6_
  7.8 9.1 %prep.1 = (bf16[256,768]{1,0:T(8,128)(2,1)}, bf16[512,768]{1,0:T(8,128)(2,1)}, bf16[512,768]{1,0:T(8,128)(2,1)}, bf16[2,768,128]{2,1,0:T(8,128)(2,1)}, f32[2,16,...) custom-call(bf16[3,128,768]{2,1,0:T(8,128)(2,1)} %refs_1_.3, ...), custom_call_target="tpu_custom_call" | custom-call | flops 4000000000 | tf_op jit(solution)/shard_map/prep/pallas_call | solution.py:69
  16.8 0.0 collective-permute-done.refs_3_
  16.8 0.0 collective-permute-done.1.refs_4_
  16.8 0.1 collective-permute-start.4
  16.9 0.5 collective-permute-start.5
  17.4 2.6 %collective-permute-done.3.refs_5_ = bf16[128,768]{1,0:T(8,128)(2,1)} collective-permute-done((bf16[128,768]{1,0:T(8,128)(2,1)}, bf16[128,768]{1,0:T(8,128)(2,1)}, u32[]{:S(2)}, u32[]{:S(2)}) %collective-permute-start.3) | collective-permute-done | bytes 196640 | tf_op jit(solution)/shard_map/ppermute | solution.py:765
  20.0 0.0 collective-permute-done.4.refs_7_
  20.0 0.0 collective-permute-done.5.refs_8_
  20.0 36.2 %main.1 = (bf16[2,128,768]{2,1,0:T(8,128)(2,1)}, bf16[128,768]{1,0:T(8,128)(2,1)}, f32[4,128,768]{2,1,0:T(8,128)}, bf16[4,128,768]{2,1,0:T(8,128)(2,1)}, bf16[32,128]{1,0:T(8,128)(2,1)}) custom-call(s32[3]{0:T(128)} %refs_0_.5, bf16[3,128,768]{2,1,0:T(8,128)(2,1)} %refs_1_.3, bf16[3,128,768]{2,1,0:T(8,128)(2,1)} %refs_2_.3, ...), custom_call_target="tpu_custom_call" | custom-call | flops 28000000000 | tf_op jit(solution)/shard_map/main/pallas_call | solution.py:69
  56.2 0.1 collective-permute-start.6
  56.3 1.8 %collective-permute-start.8 = (bf16[128,768]{1,0:T(8,128)(2,1)}, bf16[128,768]{1,0:T(8,128)(2,1)}, u32[]{:S(2)}, u32[]{:S(2)}) collective-permute-start(bf16[128,768]{1,0:T(8,128)(2,1)} %get-tuple-element.63), channel_id=1, source_target_pairs={{0,2},{1,3},{2,0},{3,1},{4,6},{5,7},{6,4},{7,5},{8,10},{9,11},{10,... | collective-permute-start | bytes 589832 | tf_op jit(solution)/shard_map/ppermute | solution.py:896
  58.1 0.2 collective-permute-start.7
  58.3 1.3 %collective-permute-done.7.refs_3_ = bf16[32,128]{1,0:T(8,128)(2,1)} collective-permute-done((bf16[32,128]{1,0:T(8,128)(2,1)}, bf16[32,128]{1,0:T(8,128)(2,1)}, u32[]{:S(2)}, u32[]{:S(2)}) %collective-permute-start.7) | collective-permute-done | bytes 8224 | tf_op jit(solution)/shard_map/ppermute | solution.py:885
  59.7 0.0 collective-permute-done.6.refs_1_.refs_2_
  59.7 2.8 %middle.1 = (bf16[2,128,768]{2,1,0:T(8,128)(2,1)}, bf16[32,16,128]{2,1,0:T(8,128)(2,1)}) custom-call(f32[4,128,768]{2,1,0:T(8,128)} %get-tuple-element.59.refs_0_.refs_1_, bf16[4,128,768]{2,1,0:T(8,128)(2,1)} %collective-permute-done.6.refs_1_.refs_2_, bf16[32,128]{1,0:T(8,128)(2,1)} %get-tuple-element.61.refs_2_, bf16[32,128]{1,0:T(8,128)(2,1)} %collective-permute-done.7.refs_3_), custom_call_target="tpu_custom_call" | custom-call | tf_op jit(solution)/shard_map/middle/pallas_call | solution.py:69
  62.5 1.1 %collective-permute-start.9 = (bf16[2,128,768]{2,1,0:T(8,128)(2,1)}, bf16[2,128,768]{2,1,0:T(8,128)(2,1)}, u32[]{:S(2)}, u32[]{:S(2)}) collective-permute-start(bf16[2,128,768]{2,1,0:T(8,128)(2,1)} %get-tuple-element.65), channel_id=1, source_target_pairs={{0,2},{1,3},{2,0},{3,1},{4,6},{5,7},{6,4},{7,5},{8,10},{9,11},{10,... | collective-permute-start | bytes 1179656 | tf_op jit(solution)/shard_map/ppermute | solution.py:895
  63.6 0.4 collective-permute-done.8.refs_5_
  63.9 14.4 %all_to_all.5.refs_0_ = bf16[32,16,128]{2,1,0:T(8,128)(2,1)} all-to-all(bf16[32,16,128]{2,1,0:T(8,128)(2,1)} %get-tuple-element.64), channel_id=1, replica_groups=mesh['dp'=8,'mp'=4] {'dp','mp'}, dimensions={0} | all-to-all | bytes 262144 | tf_op jit(solution)/shard_map/all_to_all | solution.py:898
  78.4 0.0 collective-permute-done.9.refs_3_
  78.4 3.8 %finish.1 = (f32[1,1]{1,0:T(1,128)}, bf16[3,128,768]{2,1,0:T(8,128)(2,1)}, f32[3,128,768]{2,1,0:T(8,128)}, f32[6,128]{1,0:T(8,128)}, f32[6,128]{1,0:T(8,128)}, /...) custom-call(bf16[32,16,128]{2,1,0:T(8,128)(2,1)} %all_to_all.5.refs_, ...), custom_call_target="tpu_custom_call" | custom-call | tf_op jit(solution)/shard_map/finish/pallas_call | solution.py:69
Async XLA Ops:
  0.6 7.1 %collective-permute-start.2 = (bf16[3,128,768]{2,1,0:T(8,128)(2,1)}, bf16[3,128,768]{2,1,0:T(8,128)(2,1)}, u32[]{:S(2)}, u32[]{:S(2)}) collective-permute-start(bf16[3,128,768]{2,1,0:T(8,128)(2,1)} %refs_1_.3), channel_id=1, source_target_pairs={{0,1},{1,0},{2,3},{3,2},{4,5},{5,4},{6,7},{7,6},{8,9},{9,8},{10,11... | collective-permute-start | bytes 1769480 | tf_op jit(solution)/shard_map/ppermute | solution.py:766
  3.1 13.7 %collective-permute-start = (bf16[128,768]{1,0:T(8,128)(2,1)}, bf16[128,768]{1,0:T(8,128)(2,1)}, u32[]{:S(2)}, u32[]{:S(2)}) collective-permute-start(bf16[128,768]{1,0:T(8,128)(2,1)} %get-tuple-element.45), channel_id=1, source_target_pairs={{0,2},{1,3},{2,0},{3,1},{4,6},{5,7},{6,4},{7,5},{8,10},{9,11},{10,... | collective-permute-start | bytes 589832 | tf_op jit(solution)/shard_map/ppermute | solution.py:763
  5.7 11.1 %collective-permute-start.1 = (bf16[128,768]{1,0:T(8,128)(2,1)}, bf16[128,768]{1,0:T(8,128)(2,1)}, u32[]{:S(2)}, u32[]{:S(2)}) collective-permute-start(bf16[128,768]{1,0:T(8,128)(2,1)} %get-tuple-element.46), channel_id=1, source_target_pairs={{0,2},{1,3},{2,0},{3,1},{4,6},{5,7},{6,4},{7,5},{8,10},{9,11},{10,... | collective-permute-start | bytes 589832 | tf_op jit(solution)/shard_map/ppermute | solution.py:764
  5.8 14.2 %collective-permute-start.3 = (bf16[128,768]{1,0:T(8,128)(2,1)}, bf16[128,768]{1,0:T(8,128)(2,1)}, u32[]{:S(2)}, u32[]{:S(2)}) collective-permute-start(bf16[128,768]{1,0:T(8,128)(2,1)} %get-tuple-element.50), channel_id=1, source_target_pairs={{0,2},{1,3},{2,0},{3,1},{4,6},{5,7},{6,4},{7,5},{8,10},{9,11},{10,... | collective-permute-start | bytes 589832 | tf_op jit(solution)/shard_map/ppermute | solution.py:765
  16.8 3.2 %collective-permute-start.4 = (bf16[128,768]{1,0:T(8,128)(2,1)}, bf16[128,768]{1,0:T(8,128)(2,1)}, u32[]{:S(2)}, u32[]{:S(2)}) collective-permute-start(bf16[128,768]{1,0:T(8,128)(2,1)} %collective-permute-done.refs_3_), channel_id=1, source_target_pairs={{0,1},{1,0},{2,3},{3,2},{4,5},{5,4},{6,7},{7,6},{8,9},{9,8},{10,11... | collective-permute-start | bytes 589832 | tf_op jit(solution)/shard_map/ppermute | solution.py:801
  16.9 3.1 %collective-permute-start.5 = (bf16[128,768]{1,0:T(8,128)(2,1)}, bf16[128,768]{1,0:T(8,128)(2,1)}, u32[]{:S(2)}, u32[]{:S(2)}) collective-permute-start(bf16[128,768]{1,0:T(8,128)(2,1)} %collective-permute-done.1.refs_4_), channel_id=1, source_target_pairs={{0,1},{1,0},{2,3},{3,2},{4,5},{5,4},{6,7},{7,6},{8,9},{9,8},{10,11... | collective-permute-start | bytes 589832 | tf_op jit(solution)/shard_map/ppermute | solution.py:802
  56.2 3.4 %collective-permute-start.6 = (bf16[4,128,768]{2,1,0:T(8,128)(2,1)}, bf16[4,128,768]{2,1,0:T(8,128)(2,1)}, u32[]{:S(2)}, u32[]{:S(2)}) collective-permute-start(bf16[4,128,768]{2,1,0:T(8,128)(2,1)} %get-tuple-element.60), channel_id=1, source_target_pairs={{0,1},{1,0},{2,3},{3,2},{4,5},{5,4},{6,7},{7,6},{8,9},{9,8},{10,11... | collective-permute-start | bytes 2359304 | tf_op jit(solution)/shard_map/ppermute | solution.py:884
  56.3 7.6 %collective-permute-start.8 = (bf16[128,768]{1,0:T(8,128)(2,1)}, bf16[128,768]{1,0:T(8,128)(2,1)}, u32[]{:S(2)}, u32[]{:S(2)}) collective-permute-start(bf16[128,768]{1,0:T(8,128)(2,1)} %get-tuple-element.63), channel_id=1, source_target_pairs={{0,2},{1,3},{2,0},{3,1},{4,6},{5,7},{6,4},{7,5},{8,10},{9,11},{10,... | collective-permute-start | bytes 589832 | tf_op jit(solution)/shard_map/ppermute | solution.py:896
  58.1 1.5 %collective-permute-start.7 = (bf16[32,128]{1,0:T(8,128)(2,1)}, bf16[32,128]{1,0:T(8,128)(2,1)}, u32[]{:S(2)}, u32[]{:S(2)}) collective-permute-start(bf16[32,128]{1,0:T(8,128)(2,1)} %get-tuple-element.61.refs_2_), channel_id=1, source_target_pairs={{0,1},{1,0},{2,3},{3,2},{4,5},{5,4},{6,7},{7,6},{8,9},{9,8},{10,11... | collective-permute-start | bytes 24584 | tf_op jit(solution)/shard_map/ppermute | solution.py:885
  62.5 15.9 %collective-permute-start.9 = (bf16[2,128,768]{2,1,0:T(8,128)(2,1)}, bf16[2,128,768]{2,1,0:T(8,128)(2,1)}, u32[]{:S(2)}, u32[]{:S(2)}) collective-permute-start(bf16[2,128,768]{2,1,0:T(8,128)(2,1)} %get-tuple-element.65), channel_id=1, source_target_pairs={{0,2},{1,3},{2,0},{3,1},{4,6},{5,7},{6,4},{7,5},{8,10},{9,11},{10,... | collective-permute-start | bytes 1179656 | tf_op jit(solution)/shard_map/ppermute | solution.py:895
